TPU v7x, 256 devices: a whole 4x4x8 slice. The times are simulated.
256 devices in a mesh: node: 32 (over x, y, core), rows: 8 (over z).
Axes of the slice: x: 4, y: 4, z: 8, core: 2. Of those that a mesh axis runs over, the one named last changes fastest.
Arguments:
- embeddings: bfloat16 [524288, 1024], P(('node', 'rows'))
- membership: int32 [8192, 1], P(('node', 'rows')), may hold values from 0 to 31; in each aligned block of 32 rows (0 to 31, 32 to 63, ...) at most 2 rows name the same one
- start: float32 [32, 16, 1024], P('node'), may hold values from -6 to 6
Outputs:
- directions: float32 [32, 16, 1024], P('node')
- coords: bfloat16 [16, 524288], P(None, ('node', 'rows'))
Inputs may be any that keep to these rules, and one draw needn't show every extreme that they name: `membership`: the 32 blocks of one device name each node at most 2 times; some node is named exactly 2 times; every node is named by some block.
All inputs are finite; a program needn't handle non-finite values.
Results may differ from a plain program's by a relative error of at most 0.0015.
Values may be sent and summed in bfloat16 or wider, within the bound.
A program may use at most 64 MiB of HBM per device.

v0:
```python
import jax
import jax.numpy as jnp
from jax import lax
from jax.sharding import PartitionSpec as P

PASSES = 3


def orthonormal(matrix):
    square = jnp.dot(matrix, matrix.T, precision=lax.Precision.HIGHEST)
    factor = jnp.linalg.cholesky(square)
    return lax.linalg.triangular_solve(factor, matrix, left_side=True, lower=True)


def on_device(embeddings, membership, start):
    groups = lax.axis_size("node")
    member = membership[:, 0]
    rows_here, width = embeddings.shape
    blocks_here = member.shape[0]
    most_slots = max(2, blocks_here // groups)
    block_rows = rows_here // blocks_here
    local = embeddings.reshape(blocks_here, block_rows, width)
    positions = jnp.arange(blocks_here, dtype=jnp.int32)
    same_node = member[:, None] == member[None, :]
    slot_rank = jnp.sum(
        (same_node & (positions[None, :] < positions[:, None])).astype(jnp.int32), axis=1
    )
    target = member * most_slots + slot_rank
    slot_ids = jnp.arange(groups * most_slots, dtype=jnp.int32)
    matched = target[None, :] == slot_ids[:, None]
    filled = jnp.any(matched, axis=1)
    source = jnp.sum(jnp.where(matched, positions[None, :], 0), axis=1)
    outgoing = jnp.where(filled[:, None, None], local[source], jnp.zeros((), jnp.bfloat16))
    outgoing = outgoing.reshape(groups, most_slots, block_rows, width)
    flags = filled.astype(jnp.bfloat16).reshape(groups, most_slots)
    arrived, arrived_flags = (
        lax.all_to_all(outgoing, "node", split_axis=0, concat_axis=0, tiled=True),
        lax.all_to_all(flags, "node", split_axis=0, concat_axis=0, tiled=True),
    )
    flattened = arrived.reshape(groups * most_slots * block_rows, width)
    gram_sum = lax.dot_general(
        flattened, flattened, (((0,), (0,)), ((), ())), preferred_element_type=jnp.float32
    )
    ones_row = jnp.ones((1, flattened.shape[0]), jnp.bfloat16)
    row_sum = jnp.dot(ones_row, flattened, preferred_element_type=jnp.float32)[0]
    node_size = jnp.sum(arrived_flags.astype(jnp.float32)) * block_rows
    vectors = start[0]
    gram_sum, row_sum, node_size = lax.psum((gram_sum, row_sum, node_size), "rows")
    mean = row_sum / node_size
    cov = gram_sum / node_size - mean[:, None] * mean[None, :]
    for sweep in range(PASSES):
        vectors = orthonormal(jnp.dot(vectors, cov, precision=lax.Precision.HIGHEST))
    shifted = jnp.dot(vectors, mean, precision=lax.Precision.HIGHEST)
    received = arrived.reshape(groups * most_slots, block_rows, width).astype(jnp.float32)
    values = (
        jnp.einsum("kd,srd->skr", vectors, received, precision=lax.Precision.HIGHEST)
        - shifted[None, :, None]
    )
    values = values.astype(jnp.bfloat16).reshape(groups, most_slots, vectors.shape[0], block_rows)
    returned = lax.all_to_all(values, "node", split_axis=0, concat_axis=0, tiled=True)
    mine = returned.reshape(groups * most_slots, vectors.shape[0], block_rows)[target]
    coords = mine.transpose(1, 0, 2).reshape(vectors.shape[0], blocks_here * block_rows)
    return (vectors[None], coords)


def solution(mesh):
    return jax.shard_map(
        on_device,
        mesh=mesh,
        in_specs=(P(("node", "rows"), None), P(("node", "rows"), None), P("node", None, None)),
        out_specs=(P("node", None, None), P(None, ("node", "rows"))),
        check_vma=False,
    )
```

profile of v0, /device:TPU:1, one launch (start us, length us, event | category | flops | bytes accessed | tf_op | source)
XLA Modules:
  0.0 317.7 jit_solution(2859775642732709297)
XLA Ops:
  7.2 0.9 convert_reduce_fusion.1
  8.1 0.7 multiply_add_fusion
  9.1 7.6 %gather_fusion = bf16[64,64,1024]{2,1,0:T(8,128)(2,1)} fusion(bf16[32,64,1024]{2,1,0:T(8,128)(2,1)} %bitcast.88, s32[1024]{0:T(1024)S(1)} %pad_clamp_fusion.1), kind=kCustom, calls=%fused_computation | custom fusion | bytes 16777472 | tf_op jit(solution)/shard_map/gather | solution.py:33
  16.7 7.2 %broadcast_select_fusion = bf16[32,2,64,1024]{3,2,1,0:T(8,128)(2,1)} fusion(bf16[32,2,64,1024]{3,2,1,0:T(8,128)(2,1)} %bitcast.87, pred[32,2]{1,0:T(8,128)(4,1)S(1)} %broadcast_in_dim.44), kind=kLoop, calls=%fused_computation.2 | loop fusion | flops 4194304 | bytes 16777280 | tf_op jit(solution)/shard_map/jit(_where)/select_n | solution.py:33
  23.9 104.1 %all_to_all.16 = bf16[32,2,64,1024]{3,2,1,0:T(8,128)(2,1)S(1)} all-to-all(bf16[32,2,64,1024]{3,2,1,0:T(8,128)(2,1)} %broadcast_select_fusion), channel_id=1, replica_groups=mesh['node'=32,'rows'=8] {'node'}, dimensions={0} | all-to-all | bytes 16777216 | tf_op jit(solution)/shard_map/all_to_all | solution.py:37
  128.1 3.2 %copy-done.1 = bf16[32,2,64,1024]{3,2,1,0:T(8,128)(2,1)} copy-done((bf16[32,2,64,1024]{3,2,1,0:T(8,128)(2,1)}, bf16[32,2,64,1024]{3,2,1,0:T(8,128)(2,1)S(1)}, u32[]{:S(2)}) %copy-start.1) | copy-done | bytes 8388632
  131.3 10.5 %convolution_bitcast_fusion = f32[1024,1024]{1,0:T(8,128)} fusion(bf16[32,2,64,1024]{3,2,1,0:T(8,128)(2,1)S(1)} %all_to_all.16), kind=kOutput, calls=%fused_computation.4 | convolution fusion | flops 8589934592 | bytes 12582912 | tf_op jit(solution)/shard_map/dot_general | solution.py:41
  141.9 10.7 %all_to_all.17 = bf16[32,1,2]{2,1,0:T(2,128)(2,1)S(1)} all-to-all(bf16[32,1,2]{2,1,0:T(2,128)(2,1)S(1)} %reshape.123), channel_id=1, replica_groups=mesh['node'=32,'rows'=8] {'node'}, dimensions={0} | all-to-all | bytes 256 | tf_op jit(solution)/shard_map/all_to_all | solution.py:38
  153.9 4.6 %fusion.19 = f32[1,1024]{1,0:T(1,128)S(1)} fusion(bf16[4096,1024]{1,0:T(8,128)(2,1)} %bitcast.85), kind=kOutput, calls=%fused_computation.37 | convolution fusion | flops 8388608 | bytes 8392704 | tf_op jit(solution)/shard_map/dot_general | solution.py:45
  158.5 19.9 %all-reduce = (f32[1024]{0:T(1024)S(1)}, f32[]{:T(128)}) all-reduce(f32[1024]{0:T(1024)S(1)} %bitcast.94, f32[]{:T(128)S(6)} %mul.33), channel_id=1, replica_groups=mesh['node'=32,'rows'=8] {'rows'}, use_global_device_ids=true, to_apply=%region_6.7 | all-reduce | flops 1025 | bytes 8200 | tf_op jit(solution)/shard_map/psum | solution.py:48
  178.4 0.6 broadcast_divide_fusion
  179.1 71.7 %all-reduce.3.cloned.1.call-done = f32[1024,1024]{1,0:T(8,128)} async-done(((f32[1024,1024]{1,0:T(8,128)}), f32[1024,1024]{1,0:T(8,128)}) %all-reduce.3.cloned.1.call-update) | async-done | bytes 4194320 | tf_op jit(solution)/shard_map/psum | solution.py:48
  250.7 3.4 %multiply_subtract_fusion = f32[1024,1024]{1,0:T(8,128)S(1)} fusion(f32[1024,1024]{1,0:T(8,128)} %all-reduce.3.cloned.1.call-done, f32[1024]{0:T(1024)S(1)} %broadcast_divide_fusion, f32[]{:T(128)} %get-tuple-element.5), kind=kLoop, calls=%fused_computation.3 | loop fusion | flops 3145728 | bytes 8392708 | tf_op jit(solution)/shard_map/sub | solution.py:50
  254.1 2.0 copy-done.2
  256.0 2.3 fusion.4
  258.6 1.5 cholesky.59
  260.8 0.6 fusion.8
  261.4 1.2 custom-call.7
  262.9 4.3 %fusion.29 = f32[16,1024]{1,0:T(8,128)S(1)} fusion(f32[16,1024]{1,0:T(8,128)S(1)} %fusion.2, f32[1024,1024]{1,0:T(8,128)} %copy-done.2), kind=kOutput, calls=%fused_computation.60 | convolution fusion | flops 201326592 | bytes 4325376 | tf_op jit(solution)/shard_map/dot_general | solution.py:52
  267.5 1.5 cholesky.70
  269.0 0.6 compare_reduce_fusion.1
  269.7 0.6 fusion.9
  270.3 1.2 custom-call.8
  271.8 4.3 %fusion.31 = f32[16,1024]{1,0:T(8,128)S(1)} fusion(f32[16,1024]{1,0:T(8,128)S(1)} %fusion.14, f32[1024,1024]{1,0:T(8,128)} %copy-done.2), kind=kOutput, calls=%fused_computation.62 | convolution fusion | flops 201326592 | bytes 4325376 | tf_op jit(solution)/shard_map/dot_general | solution.py:52
  276.4 1.5 cholesky.81
  278.5 0.6 fusion.10
  279.2 1.2 custom-call.9
  280.9 12.2 %fusion = bf16[64,64,16]{1,2,0:T(8,128)(2,1)S(1)} fusion(bf16[64,64,1024]{2,1,0:T(8,128)(2,1)} %bitcast.86, f32[16]{0:T(128)S(1)} %convolution_bitcast_fusion.1, f32[16,1024]{1,0:T(8,128)S(1)} %fusion.11), kind=kOutput, calls=%fused_computation.6 | convolution fusion | flops 805437440 | bytes 8585280 | tf_op jit(solution)/shard_map/kd,srd->skr/dot_general | solution.py:56
  293.1 0.8 reshape.124
  293.9 7.5 %all-to-all-start.2 = ((bf16[32,2,1024]{2,1,0:T(2,128)(2,1)}), bf16[32,2,1024]{2,1,0:T(2,128)(2,1)S(1)}, u32[]{:S(2)}, u32[]{:S(2)}) async-start(bf16[32,2,1024]{2,1,0:T(2,128)(2,1)} %reshape.124), calls=%async_computation.2 | async-start | bytes 262144 | tf_op jit(solution)/shard_map/all_to_all | solution.py:60
  301.5 7.7 %all-to-all-done.2 = bf16[32,2,1024]{2,1,0:T(2,128)(2,1)S(1)} async-done(((bf16[32,2,1024]{2,1,0:T(2,128)(2,1)}), bf16[32,2,1024]{2,1,0:T(2,128)(2,1)S(1)}, u32[]{:S(2)}, u32[]{:S(2)}) %all-to-all-start.2) | async-done | bytes 131104 | tf_op jit(solution)/shard_map/all_to_all | solution.py:60
  310.0 0.8 reshape.89
  (41 shorter events, 5.1 us)
Async XLA Ops:
  7.2 248.9 %copy-start = (f32[1,16,1024]{2,1,0:T(8,128)S(1)}, f32[1,16,1024]{2,1,0:T(8,128)}, u32[]{:S(2)}) copy-start(f32[1,16,1024]{2,1,0:T(8,128)} %param.8) | copy-start | bytes 196612
  7.2 243.5 %all-reduce.3.cloned.1.call-start = ((), (), s32[]{:S(2)}) async-start(), calls=%async_computation.3 | async-start | bytes 8388608 | tf_op jit(solution)/shard_map/psum | solution.py:48
  128.1 3.2 %copy-start.1 = (bf16[32,2,64,1024]{3,2,1,0:T(8,128)(2,1)}, bf16[32,2,64,1024]{3,2,1,0:T(8,128)(2,1)S(1)}, u32[]{:S(2)}) copy-start(bf16[32,2,64,1024]{3,2,1,0:T(8,128)(2,1)S(1)} %all_to_all.16) | copy-start | bytes 25165828
  254.1 2.0 copy-start.2
  280.7 12.4 %copy-start.3 = (f32[16,1024]{1,0:T(8,128)}, f32[16,1024]{1,0:T(8,128)S(1)}, u32[]{:S(2)}) copy-start(f32[16,1024]{1,0:T(8,128)S(1)} %fusion.11) | copy-start | bytes 196612
  280.9 20.6 %copy-start.4 = (s32[32,1]{0,1:T(1,128)S(1)}, s32[32,1]{0,1:T(1,128)}, u32[]{:S(2)}) copy-start(s32[32,1]{0,1:T(1,128)} %param.7) | copy-start | bytes 388
  293.9 15.2 %all-to-all-start.2 = ((bf16[32,2,1024]{2,1,0:T(2,128)(2,1)}), bf16[32,2,1024]{2,1,0:T(2,128)(2,1)S(1)}, u32[]{:S(2)}, u32[]{:S(2)}) async-start(bf16[32,2,1024]{2,1,0:T(2,128)(2,1)} %reshape.124), calls=%async_computation.2 | async-start | bytes 262144 | tf_op jit(solution)/shard_map/all_to_all | solution.py:60
Sparse Core Ops, SparseCore 0:
  141.9 108.7 all-reduce.2
where the time goes:
time: 318 us
  blocking collectives  135 us (42%)
  waiting for transfers between devices  79.3 us (25%)
  matrix products  39.5 us (12%)
  other arithmetic  25.8 us (8%)
  local copies, waits for them, and re-layouts  15.8 us (5%)
  between operations  14.9 us (5%)
  starting transfers between devices  7.57 us (2%)
    all_to_all x1, blocking collectives, on_device(): lax.all_to_all(outgoing, 'node', split_axis=0, concat_axis=0, tiled=True)  104 us
    psum x1, waiting for transfers between devices, on_device(): lax.psum((gram_sum, row_sum, node_size), 'rows')  71.7 us
    psum x1, blocking collectives, on_device(): lax.psum((gram_sum, row_sum, node_size), 'rows')  19.9 us
    dot_general x1, matrix products, on_device(): jnp.einsum('kd,srd->skr', vectors, received, precision=lax.Precision.HIGH...  12.2 us
    dot_general x3, matrix products, on_device(): jnp.dot(vectors, cov, precision=lax.Precision.HIGHEST)  10.9 us
    all_to_all x1, blocking collectives, on_device(): lax.all_to_all(flags, 'node', split_axis=0, concat_axis=0, tiled=True)  10.7 us
    dot_general x1, matrix products, on_device(): lax.dot_general(flattened, flattened, (((0,), (0,)), ((), ())), preferred...  10.5 us
    all_to_all x1, waiting for transfers between devices, on_device(): lax.all_to_all(values, 'node', split_axis=0, concat_axis=0, tiled=True)  7.67 us
  transfers between devices with their start and end apart: 2, of which 2 were waited for; matrix products, arithmetic and copies ran while one was open for 2% of the time, Pallas kernels for 0%

commit v1 on v0

v1 whole, which is shorter than its diff:
```python
import functools

import jax
import jax.numpy as jnp
from jax import lax
from jax.experimental import pallas as pl
from jax.experimental.pallas import tpu as pltpu
from jax.sharding import PartitionSpec as P

PASSES = 3
MESH = pl.DeviceIdType.MESH
F32 = jnp.float32
BF16 = jnp.bfloat16

DIRS = 16
D = 1024
EXT = 128
WIDE = D + EXT
CUT = 640
ROWS = 2048
BLOCK = 64
BLOCKS = 32
TILE = 256
PER = TILE // BLOCK
NX, NY, NZ = 4, 4, 8


def split3(v):
    hi = v.astype(BF16)
    rest = v - hi.astype(F32)
    mid = rest.astype(BF16)
    lo = (rest - mid.astype(F32)).astype(BF16)
    return hi, mid, lo


def kernel(
    member, first, second, x_hbm, start, dirs, coords,
    xv, vall, wblk, acc, sendc, recvc, r1, r2, b1, b2, r3, r4, cc, r5, r6, ff,
    xsem, ag_a1s, ag_a1r, ag_a2s, ag_a2r, ag_b1s, ag_b1r, ag_b2s, ag_b2r, ag_cs, ag_cr,
    rs_cs, rs_cr, rs_1s, rs_1r, rs_2s, rs_2r, rs_3s, rs_3r, rs_4s, rs_4r,
    z_1s, z_1r, z_2s, z_2r, z_3s, z_3r,
):
    me = lax.axis_index("node")
    z = lax.axis_index("rows")
    x, y, c = me // 8, (me // 2) % 4, me % 2

    def at(x_, y_, c_):
        return (x_ * 8 + y_ * 2 + c_, z)

    def along_x(d):
        return at((x + d) % NX, y, c)

    def along_y(d):
        return at(x, (y + d) % NY, c)

    def along_z(d):
        return (me, (z + d) % NZ)

    partner = at(x, y, 1 - c)

    def send(src, dst, ssem, rsem, to):
        return pltpu.make_async_remote_copy(
            src_ref=src, dst_ref=dst, send_sem=ssem, recv_sem=rsem, device_id=to, device_id_type=MESH
        )

    load = pltpu.make_async_copy(x_hbm, xv, xsem)
    load.start()

    barrier = pltpu.get_barrier_semaphore()
    peers = [partner]
    peers += [along_x(d) for d in range(1, NX)]
    peers += [along_y(d) for d in range(1, NY)]
    peers += [along_z(d) for d in range(1, NZ)]
    for peer in peers:
        pl.semaphore_signal(barrier, inc=1, device_id=peer, device_id_type=MESH)
    pl.semaphore_wait(barrier, len(peers))

    vall[x, y, c, :, 0:D] = start[...]
    vall[x, y, c, :, D:WIDE] = jnp.zeros((DIRS, EXT), F32)
    wblk[BLOCKS] = jnp.zeros((DIRS, WIDE), F32)

    def gather():
        one = lambda a, b, lo, hi: vall.at[a, b, c, :, lo:hi]
        row = lambda a: vall.at[a, :, c, :, 0:CUT]
        col = lambda b: vall.at[:, b, c, :, CUT:WIDE]
        sent, core = [], []
        for d in range(1, 4):
            own = one(x, y, 0, CUT)
            sent.append(send(own, own, ag_a1s.at[d - 1], ag_a1r.at[d - 1], along_y(d)))
            own = one(x, y, CUT, WIDE)
            sent.append(send(own, own, ag_a2s.at[d - 1], ag_a2r.at[d - 1], along_x(d)))
        for cp in sent:
            cp.start()

        def hand(ref):
            i = len(core)
            core.append(send(ref, ref, ag_cs.at[i], ag_cr.at[i], partner))
            core[-1].start()

        hand(vall.at[x, y, c])
        for cp in sent:
            cp.wait_recv()
        later = []
        for d in range(1, 4):
            later.append(send(row(x), row(x), ag_b1s.at[d - 1], ag_b1r.at[d - 1], along_x(d)))
            later.append(send(col(y), col(y), ag_b2s.at[d - 1], ag_b2r.at[d - 1], along_y(d)))
        for cp in later:
            cp.start()
        for d in range(1, 4):
            hand(one(x, (y - d) % NY, 0, CUT))
            hand(one((x - d) % NX, y, CUT, WIDE))
        for d in range(1, 4):
            later[2 * d - 2].wait_recv()
            hand(row((x - d) % NX))
            later[2 * d - 1].wait_recv()
            hand(col((y - d) % NY))
        for cp in core:
            cp.wait_recv()
        for cp in sent + later + core:
            cp.wait_send()

    group = lax.broadcasted_iota(jnp.int32, (DIRS, TILE), 1) >> 6

    def project(t):
        tile = xv[pl.ds(pl.multiple_of(t * TILE, TILE), TILE), :]
        parts, shifts = [], []
        for i in range(PER):
            m = member[PER * t + i]
            parts += split3(vall[m // 8, (m // 2) % 4, m % 2, :, 0:D])
            shifts.append(vall[m // 8, (m // 2) % 4, m % 2, :, D:WIDE])
        stack = jnp.concatenate(parts, axis=0)
        p3 = lax.dot_general(stack, tile, (((1,), (1,)), ((), ())), preferred_element_type=F32)
        out = []
        for i in range(PER):
            a = 3 * DIRS * i
            p = (p3[a + 2 * DIRS : a + 3 * DIRS] + p3[a + DIRS : a + 2 * DIRS]) + p3[a : a + DIRS]
            p = p - jnp.concatenate([shifts[i], shifts[i]], axis=1)
            out.append(jnp.where(group == i, p, 0.0))
        return tile, out

    ones_rows = (
        lax.broadcasted_iota(jnp.int32, (DIRS, TILE), 0) == group
    ).astype(F32).astype(BF16)

    def tile_step(t, carry):
        tile, ps = project(t)
        stack = []
        for p in ps:
            stack += split3(p)
        stack.append(ones_rows)
        w3 = jnp.dot(jnp.concatenate(stack, axis=0), tile, preferred_element_type=F32)
        for i in range(PER):
            a = 3 * DIRS * i
            b = PER * t + i
            wblk[b, :, 0:D] = (
                w3[a + 2 * DIRS : a + 3 * DIRS] + w3[a + DIRS : a + 2 * DIRS]
            ) + w3[a : a + DIRS]
            s = 3 * DIRS * PER + i
            for r in range(8):
                wblk[b, r : r + 1, D:WIDE] = w3[s : s + 1, 128 * r : 128 * (r + 1)]
            wblk[b, 8:16, D:WIDE] = jnp.full((8, EXT), float(BLOCK), F32)
        return carry

    def scatter():
        def for_partner(i, carry):
            a, b = i // NY, i % NY
            j = i * 2 + (1 - c)
            sendc[a, b] = wblk[first[j]] + wblk[second[j]]
            return carry

        def for_own(i, carry):
            a, b = i // NY, i % NY
            j = i * 2 + c
            acc[a, b] = wblk[first[j]] + wblk[second[j]]
            return carry

        lax.fori_loop(0, 16, for_partner, 0)
        over = send(sendc, recvc, rs_cs, rs_cr, partner)
        over.start()
        lax.fori_loop(0, 16, for_own, 0)
        over.wait_recv()

        def add_core(i, carry):
            a, b = i // NY, i % NY
            acc[a, b] = acc[a, b] + recvc[a, b]
            return carry

        lax.fori_loop(0, 16, add_core, 0)
        sent = []
        for d in range(1, 4):
            sent.append(send(acc.at[(x + d) % NX, :, :, 0:CUT], r1.at[d - 1],
                             rs_1s.at[d - 1], rs_1r.at[d - 1], along_x(d)))
            sent.append(send(acc.at[:, (y + d) % NY, :, CUT:WIDE], r2.at[d - 1],
                             rs_2s.at[d - 1], rs_2r.at[d - 1], along_y(d)))
        for cp in sent:
            cp.start()
        for cp in sent:
            cp.wait_recv()
        for q in range(4):
            b1[q] = (acc[x, q, :, 0:CUT] + r1[0, q]) + (r1[1, q] + r1[2, q])
            b2[q] = (acc[q, y, :, CUT:WIDE] + r2[0, q]) + (r2[1, q] + r2[2, q])
        later = []
        for d in range(1, 4):
            later.append(send(b1.at[(y + d) % NY], r3.at[d - 1],
                              rs_3s.at[d - 1], rs_3r.at[d - 1], along_y(d)))
            later.append(send(b2.at[(x + d) % NX], r4.at[d - 1],
                              rs_4s.at[d - 1], rs_4r.at[d - 1], along_x(d)))
        for cp in later:
            cp.start()
        for cp in later:
            cp.wait_recv()
        cc[:, 0:CUT] = (b1[y] + r3[0]) + (r3[1] + r3[2])
        cc[:, CUT:WIDE] = (b2[x] + r4[0]) + (r4[1] + r4[2])
        r6[z] = cc[:, D:WIDE]
        ring = []
        for d in range(1, NZ):
            there = pl.ds(pl.multiple_of(((z + d) % NZ) * 128, 128), 128)
            ring.append(send(cc.at[:, there], r5.at[d - 1], z_1s.at[d - 1], z_1r.at[d - 1], along_z(d)))
            ring.append(send(cc.at[:, D:WIDE], r6.at[z], z_2s.at[d - 1], z_2r.at[d - 1], along_z(d)))
        for cp in ring:
            cp.start()
        for cp in ring:
            cp.wait_recv()
        here = pl.ds(pl.multiple_of(z * 128, 128), 128)
        part = cc[:, here]
        for d in range(NZ - 1):
            part = part + r5[d]
        extra = r6[0]
        for d in range(1, NZ):
            extra = extra + r6[d]
        ff[:, here] = part
        back = []
        for d in range(1, NZ):
            back.append(send(ff.at[:, here], ff.at[:, here], z_3s.at[d - 1], z_3r.at[d - 1], along_z(d)))
        for cp in back:
            cp.start()
        for cp in back:
            cp.wait_recv()
        for cp in [over] + sent + later + ring + back:
            cp.wait_send()
        return extra

    row_id = lax.broadcasted_iota(jnp.int32, (DIRS, 1), 0)

    def one_pass(step, carry):
        gather()

        @pl.when(step == 0)
        def _():
            load.wait()

        lax.fori_loop(0, ROWS // TILE, tile_step, 0)
        extra = scatter()
        size = extra[8:9, :]
        mean = extra[0:8, :] / size
        mean_row = jnp.concatenate([mean[r : r + 1] for r in range(8)], axis=1)
        size_row = jnp.concatenate([size] * 8, axis=1)
        old = vall[x, y, c, :, 0:D]
        offset = jnp.where(step == 0, jnp.sum(old * mean_row, axis=1, keepdims=True), 0.0)
        w = ff[...] / size_row - offset * mean_row
        g = lax.dot_general(w, w, (((1,), (1,)), ((), ())), precision=lax.Precision.HIGHEST,
                            preferred_element_type=F32)
        scale = jnp.zeros((DIRS, 1), F32)
        for k in range(DIRS):
            pivot = g[k : k + 1, k : k + 1]
            f = jnp.where(row_id > k, g[:, k : k + 1] / pivot, 0.0)
            scale = jnp.where(row_id == k, 1.0 / jnp.sqrt(pivot), scale)
            g = g - f * g[k : k + 1, :]
            w = w - f * w[k : k + 1, :]
        v = w * scale
        vall[x, y, c, :, 0:D] = v
        vall[x, y, c, :, D:WIDE] = jnp.broadcast_to(
            jnp.sum(v * mean_row, axis=1, keepdims=True), (DIRS, EXT)
        )
        return carry

    lax.fori_loop(0, PASSES, one_pass, 0)
    dirs[...] = vall[x, y, c, :, 0:D]
    gather()

    def last(t, carry):
        _, ps = project(t)
        coords[:, pl.ds(pl.multiple_of(t * TILE, TILE), TILE)] = (
            (ps[0] + ps[1]) + (ps[2] + ps[3])
        ).astype(BF16)
        return carry

    lax.fori_loop(0, ROWS // TILE, last, 0)


def on_device(embeddings, membership, start):
    member = membership[:, 0]
    nodes = jnp.arange(32, dtype=jnp.int32)
    blocks = jnp.arange(BLOCKS, dtype=jnp.int32)
    same = member[None, :] == nodes[:, None]
    first = jnp.min(jnp.where(same, blocks[None, :], BLOCKS), axis=1)
    second = jnp.max(jnp.where(same, blocks[None, :], -1), axis=1)
    second = jnp.where((second < 0) | (second == first), BLOCKS, second)
    smem = pl.BlockSpec(memory_space=pltpu.SMEM)
    vmem = pl.BlockSpec(memory_space=pltpu.VMEM)
    dma = pltpu.SemaphoreType.DMA
    dirs, coords = pl.pallas_call(
        kernel,
        out_shape=(
            jax.ShapeDtypeStruct((DIRS, D), F32),
            jax.ShapeDtypeStruct((DIRS, ROWS), BF16),
        ),
        in_specs=[smem, smem, smem, pl.BlockSpec(memory_space=pl.ANY), vmem],
        out_specs=(vmem, vmem),
        scratch_shapes=[
            pltpu.VMEM((ROWS, D), BF16),
            pltpu.VMEM((NX, NY, 2, DIRS, WIDE), F32),
            pltpu.VMEM((BLOCKS + 1, DIRS, WIDE), F32),
            pltpu.VMEM((NX, NY, DIRS, WIDE), F32),
            pltpu.VMEM((NX, NY, DIRS, WIDE), F32),
            pltpu.VMEM((NX, NY, DIRS, WIDE), F32),
            pltpu.VMEM((3, NY, DIRS, CUT), F32),
            pltpu.VMEM((3, NX, DIRS, WIDE - CUT), F32),
            pltpu.VMEM((NY, DIRS, CUT), F32),
            pltpu.VMEM((NX, DIRS, WIDE - CUT), F32),
            pltpu.VMEM((3, DIRS, CUT), F32),
            pltpu.VMEM((3, DIRS, WIDE - CUT), F32),
            pltpu.VMEM((DIRS, WIDE), F32),
            pltpu.VMEM((NZ - 1, DIRS, 128), F32),
            pltpu.VMEM((NZ, DIRS, EXT), F32),
            pltpu.VMEM((DIRS, D), F32),
            dma,
            dma((3,)), dma((3,)), dma((3,)), dma((3,)),
            dma((3,)), dma((3,)), dma((3,)), dma((3,)),
            dma((13,)), dma((13,)),
            dma, dma,
            dma((3,)), dma((3,)), dma((3,)), dma((3,)),
            dma((3,)), dma((3,)), dma((3,)), dma((3,)),
            dma((7,)), dma((7,)), dma((7,)), dma((7,)), dma((7,)), dma((7,)),
        ],
        compiler_params=pltpu.CompilerParams(
            collective_id=0, has_side_effects=True, vmem_limit_bytes=40 * 1024 * 1024
        ),
    )(member, first, second, embeddings, start[0])
    return (dirs[None], coords)


def solution(mesh):
    return jax.shard_map(
        on_device,
        mesh=mesh,
        in_specs=(P(("node", "rows"), None), P(("node", "rows"), None), P("node", None, None)),
        out_specs=(P("node", None, None), P(None, ("node", "rows"))),
        check_vma=False,
    )
```

time: 318 us -> 188 us (0.59)
  Pallas kernels: 0 us -> 181 us
  blocking collectives: 135 us -> 0 us
  waiting for transfers between devices: 79.3 us -> 0 us
  matrix products: 39.5 us -> 0 us
  other arithmetic: 25.8 us -> 0.78 us
  between operations: 14.9 us -> 0.65 us
  local copies, waits for them, and re-layouts: 15.8 us -> 4.94 us
  starting transfers between devices: 7.57 us -> 0 us
    pallas_call x0 -> x1, Pallas kernels: none -> 181 us  [on_device(): pl.pallas_call(kernel, out_shape=(jax.ShapeDtypeStruct((DIRS, D), F32), j...]
    all_to_all x2 -> x0, blocking collectives: 115 us -> none  [the longest x1 104 us: on_device(): lax.all_to_all(outgoing, 'node', split_axis=0, concat_axis=0, tiled=True)]
    psum x1 -> x0, waiting for transfers between devices: 71.7 us -> none  [on_device(): lax.psum((gram_sum, row_sum, node_size), 'rows')]
    dot_general x10 -> x0, matrix products: 38.7 us -> none  [the longest x1 12.2 us: on_device(): jnp.einsum('kd,srd->skr', vectors, received, precision=lax.Precision.HIGH...]
    psum x1 -> x0, blocking collectives: 19.9 us -> none  [on_device(): lax.psum((gram_sum, row_sum, node_size), 'rows')]
    another operation x15 -> x0, other arithmetic: 12.1 us -> none  [the longest x9 6.5 us: orthonormal(): factor = jnp.linalg.cholesky(square)]
    gather x2 -> x0, local copies, waits for them, and re-layouts: 8.2 us -> none  [the longest x1 7.61 us: on_device(): local[source]]
    all_to_all x1 -> x0, waiting for transfers between devices: 7.67 us -> none  [on_device(): lax.all_to_all(values, 'node', split_axis=0, concat_axis=0, tiled=True)]
  transfers between devices with their start and end apart: 2 -> 0, of which waited for: 2 -> 0; matrix products, arithmetic and copies ran while one was open for 2% -> 0% of each run, Pallas kernels for 0% -> 0%
where the time goes in v1:
time: 188 us
  Pallas kernels  181 us (96%)
  local copies, waits for them, and re-layouts  4.94 us (3%)
    pallas_call x1, Pallas kernels, on_device(): pl.pallas_call(kernel, out_shape=(jax.ShapeDtypeStruct((DIRS, D), F32), j...  181 us
    unnamed x8, local copies, waits for them, and re-layouts  4.94 us

profile of v1, /device:TPU:1, one launch (start us, length us, event | category | flops | bytes accessed | tf_op | source)
XLA Modules:
  0.0 187.5 jit_solution(1794823456060414085)
XLA Ops:
  0.6 0.8 select_reduce_fusion
  1.4 0.0 copy-start
  1.4 2.2 %copy-done = bf16[2048,1024]{1,0:T(8,128)(2,1)S(1)} copy-done((bf16[2048,1024]{1,0:T(8,128)(2,1)S(1)}, bf16[2048,1024]{1,0:T(8,128)(2,1)}, u32[]{:S(2)}) %copy-start) | copy-done | bytes 4194328
  3.6 0.0 copy-start.1
  3.6 0.8 copy-done.1
  4.4 0.0 copy-start.2
  4.5 0.7 copy-done.2
  5.1 181.1 %shard_map.50 = (f32[16,1024]{1,0:T(8,128)S(1)}, bf16[16,2048]{1,0:T(8,128)(2,1)S(1)}) custom-call(s32[32]{0:T(128)S(1)} %bitcast.6, s32[32]{0:T(128)S(1)} %get-tuple-element.7.first, s32[32]{0:T(128)S(1)} %or_select_fusion.second, bf16[2048,1024]{1,0:T(8,128)(2,1)S(1)} %copy-done, f32[16,1024]{1,0:T(8,128)S(1)} %bitcast.3), custom_call_target="tpu_custom_call" | custom-call | tf_op jit(solution)/shard_map/pallas_call | solution.py:302
  186.3 0.6 copy.7
  186.9 0.6 copy.8
  (1 shorter events, 0.0 us)
Async XLA Ops:
  1.4 2.2 %copy-start = (bf16[2048,1024]{1,0:T(8,128)(2,1)S(1)}, bf16[2048,1024]{1,0:T(8,128)(2,1)}, u32[]{:S(2)}) copy-start(bf16[2048,1024]{1,0:T(8,128)(2,1)} %x_hbm.1) | copy-start | bytes 12582916
  3.6 0.8 copy-start.1
  4.4 0.7 copy-start.2

commit v2 on v0

v2 whole, which is shorter than its diff:
```python
import jax
import jax.numpy as jnp
from jax import lax
from jax.experimental import pallas as pl
from jax.experimental.pallas import tpu as pltpu
from jax.sharding import PartitionSpec as P

PASSES = 3
MESH = pl.DeviceIdType.MESH
F32 = jnp.float32
BF16 = jnp.bfloat16
I16 = jnp.int16
I32 = jnp.int32

DIRS = 16
D = 1024
HALF = 512
LANES = 128
KT = HALF // LANES
ROWS = 2048
BLOCK = 64
BLOCKS = 32
TILE = 256
PER = TILE // BLOCK
TILES = ROWS // TILE
CHIPS = 16
NZ = 8


def code(w):
    tiles = [w[:, LANES * k : LANES * (k + 1)] for k in range(KT)]
    top = jnp.maximum(
        jnp.maximum(jnp.abs(tiles[0]), jnp.abs(tiles[1])), jnp.maximum(jnp.abs(tiles[2]), jnp.abs(tiles[3]))
    )
    top = jnp.maximum(jnp.max(top, axis=1, keepdims=True), 1e-30)
    e = jnp.floor(jnp.log2(top))
    scale = jnp.exp2(14.0 - e)
    out = [
        jnp.clip(jnp.round(t * scale), -32767.0, 32767.0).astype(I32).astype(I16) for t in tiles
    ]
    return out, jnp.broadcast_to(e.astype(I32), (DIRS, LANES)).astype(I16)


def put(ref, w):
    out, e = code(w)
    for k in range(KT):
        ref[k] = out[k]
    ref[KT] = e


def scale_of(ref):
    return jnp.exp2(ref[KT].astype(I32).astype(F32) - 14.0)


def kernel(
    member, x_hbm, start, dirs, coords,
    xh, smt, smm, mv, tab, vs, vr, vq, vhl, shift, shift0, shift1, pc, pr, wblk, wq, rq, zq, gs, gr, vout, vin,
    sblk, snode, sr, sz, mm,
    xsem, xs, xr, msem, mss, msr, nsem, tsem, vsem, vss, vsr, h_s, h_r, ag_s, ag_r, p_s, p_r, rs_s, rs_r, z_s, z_r, g_s, g_r,
    ms_s, ms_r, mz_s, mz_r, ma_s, ma_r, o_s, o_r,
):
    me = lax.axis_index("node")
    z = lax.axis_index("rows")
    x, y, c = me >> 3, (me >> 1) & 3, me & 1
    chip = me >> 1
    other = 1 - c

    def chip_at(d):
        return (((x + (d >> 2)) & 3) << 2) + ((y + d) & 3)

    def chip_from(d):
        return (((x + 4 - (d >> 2)) & 3) << 2) + ((y + 4 - (d & 3)) & 3)

    def plane(d):
        return (chip_at(d) * 2 + c, z)

    def column(d):
        return (me, (z + d) & (NZ - 1))

    partner = (chip * 2 + other, z)

    def send(src, dst, ssem, rsem, to):
        return pltpu.make_async_remote_copy(
            src_ref=src, dst_ref=dst, send_sem=ssem, recv_sem=rsem, device_id=to, device_id_type=MESH
        )

    def each(n, what):
        def body(d, carry):
            what(d)
            return carry

        lax.fori_loop(1, n, body, 0)

    mine = pl.ds(pl.multiple_of(c * HALF, HALF), HALF)
    theirs = pl.ds(pl.multiple_of(other * HALF, HALF), HALF)
    load = pltpu.make_async_copy(x_hbm.at[:, mine], xh.at[c], xsem)
    load.start()
    load_m = pltpu.make_async_copy(member, mv.at[c], msem)
    load_m.start()
    load_v = pltpu.make_async_copy(start.at[0], vs, vsem)
    load_v.start()

    barrier = pltpu.get_barrier_semaphore()
    pl.semaphore_signal(barrier, inc=1, device_id=partner, device_id_type=MESH)

    def greet_plane(d):
        pl.semaphore_signal(barrier, inc=1, device_id=plane(d), device_id_type=MESH)

    def greet_column(d):
        pl.semaphore_signal(barrier, inc=1, device_id=column(d), device_id_type=MESH)

    each(CHIPS, greet_plane)
    each(NZ, greet_column)

    group = lax.broadcasted_iota(I32, (DIRS, TILE), 1) >> 6
    ones_rows = (lax.broadcasted_iota(I32, (DIRS, TILE), 0) == group).astype(F32).astype(BF16)

    def sum_tiles(h):
        def body(t, carry):
            tile = xh[h, pl.ds(pl.multiple_of(t * TILE, TILE), TILE), :]
            s = jnp.dot(ones_rows, tile, preferred_element_type=F32)
            for i in range(PER):
                rows = [s[i : i + 1, LANES * k : LANES * (k + 1)] for k in range(KT)]
                rows.append(jnp.full((1, LANES), float(BLOCK), F32))
                rows.append(jnp.zeros((3, LANES), F32))
                sblk[h, PER * t + i] = jnp.concatenate(rows, axis=0)
            return carry

        lax.fori_loop(0, TILES, body, 0)

    wblk[0, BLOCKS] = jnp.zeros((DIRS, HALF), F32)
    wblk[1, BLOCKS] = jnp.zeros((DIRS, HALF), F32)
    sblk[0, BLOCKS] = jnp.zeros((8, LANES), F32)
    sblk[1, BLOCKS] = jnp.zeros((8, LANES), F32)
    load_v.wait()
    put(vq.at[c, chip], vs[:, mine])
    load_m.wait()
    load.wait()
    sum_tiles(c)

    pl.semaphore_wait(barrier, 1 + (CHIPS - 1) + (NZ - 1))

    over_v = send(vs.at[:, theirs], vr, vss, vsr, partner)
    over_v.start()
    over_m = send(mv.at[c], mv.at[c], mss, msr, partner)
    over_m.start()
    over_x = send(x_hbm.at[:, theirs], xh.at[c], xs, xr, partner)
    over_x.start()

    def v_copy(n, d):
        ref = vq.at[n, chip]
        return send(ref, ref, ag_s.at[n, d - 1], ag_r.at[n, d - 1], plane(d))

    def gather_start(n):
        each(CHIPS, lambda d: v_copy(n, d).start())

    gather_start(c)
    over_v.wait_recv()
    put(vq.at[other, chip], vr[...])
    gather_start(other)

    over_m.wait_recv()
    names = pltpu.make_async_copy(mv, smm, nsem)
    names.start()
    names.wait()
    lane = lax.broadcasted_iota(I32, (1, LANES), 1)
    for h in range(2):
        low = jnp.full((1, LANES), BLOCKS, I32)
        high = low
        hits = jnp.zeros((1, LANES), I32)
        for b in range(BLOCKS):
            hit = lane == smm[h, 0, b]
            low = jnp.where(hit & (hits == 0), b, low)
            high = jnp.where(hit & (hits > 0), b, high)
            hits = jnp.where(hit, hits + 1, hits)
        row = jnp.concatenate([mv[h], jnp.zeros((1, LANES - BLOCKS), I32)], axis=1)
        tab[h] = jnp.concatenate([row, low, high, jnp.zeros((5, LANES), I32)], axis=0)
    move = pltpu.make_async_copy(tab, smt, tsem)
    move.start()
    over_x.wait_recv()
    sum_tiles(other)
    move.wait()

    def total(ref, j):
        f0, s0 = smt[0, 1, j], smt[0, 2, j]
        f1, s1 = smt[1, 1, j], smt[1, 2, j]
        return (ref[0, f0] + ref[0, s0]) + (ref[1, f1] + ref[1, s1])

    def node_sums(i, carry):
        for n in range(2):
            snode[i, n] = total(sblk, 2 * i + n)
        return carry

    lax.fori_loop(0, CHIPS, node_sums, 0)
    sr[chip] = snode[chip]

    def ms(d):
        return send(snode.at[chip_at(d)], sr.at[chip], ms_s.at[d - 1], ms_r.at[d - 1], plane(d))

    def mz(d):
        return send(sz.at[z], sz.at[z], mz_s.at[d - 1], mz_r.at[d - 1], column(d))

    def ma(d):
        return send(mm.at[chip], mm.at[chip], ma_s.at[d - 1], ma_r.at[d - 1], plane(d))

    each(CHIPS, lambda d: ms(d).start())

    def sums_to_column():
        each(CHIPS, lambda d: ms(d).wait_recv())
        acc = sr[0]
        for i in range(1, CHIPS):
            acc = acc + sr[i]
        sz[z] = acc
        each(NZ, lambda d: mz(d).start())

    def means_to_plane():
        each(NZ, lambda d: mz(d).wait_recv())
        acc = sz[0]
        for i in range(1, NZ):
            acc = acc + sz[i]
        tile_row = lax.broadcasted_iota(I32, (2, 8, LANES), 1)
        mm[chip] = jnp.where(tile_row < KT, acc / acc[:, KT : KT + 1, :], acc)
        each(CHIPS, lambda d: ma(d).start())
        each(CHIPS, lambda d: ma(d).wait_recv())

    def offsets():
        def body(j, carry):
            dots = None
            for k in range(KT):
                cut = slice(LANES * k, LANES * (k + 1))
                v = vhl[j, 0:DIRS, cut].astype(F32) + vhl[j, DIRS : 2 * DIRS, cut].astype(F32)
                term = v * mm[j // 2, j % 2, k : k + 1, :]
                dots = term if dots is None else dots + term
            shift0[j] = jnp.broadcast_to(jnp.sum(dots, axis=1, keepdims=True), (DIRS, LANES))
            return carry

        lax.fori_loop(0, 32, body, 0)

    over_h = send(shift0, shift1, h_s, h_r, partner)

    def convert(n, i, first):
        ref = vq.at[n, i]
        scale = scale_of(ref)
        his, los, dots = [], [], None
        for k in range(KT):
            q = ref[k].astype(I32)
            hi = ((q >> 8) << 8).astype(F32) * scale
            lo = (q & 255).astype(F32) * scale
            his.append(hi.astype(BF16))
            los.append(lo.astype(BF16))
            if not first:
                term = (hi + lo) * mm[i, n, k : k + 1, :]
                dots = term if dots is None else dots + term
        j = 2 * i + n
        vhl[j, 0:DIRS, :] = jnp.concatenate(his, axis=1)
        vhl[j, DIRS : 2 * DIRS, :] = jnp.concatenate(los, axis=1)
        if first:
            shift[j] = jnp.zeros((DIRS, LANES), F32)
        else:
            shift[j] = jnp.broadcast_to(jnp.sum(dots, axis=1, keepdims=True), (DIRS, LANES))

    def receive(first):
        for n in range(2):
            convert(n, chip, first)

            def arrived(d):
                v_copy(n, d).wait_recv()
                convert(n, chip_from(d), first)

            each(CHIPS, arrived)

    def project(h):
        def one(t):
            at = pl.ds(pl.multiple_of(t * TILE, TILE), TILE)
            parts, shifts = [], []
            for i in range(PER):
                m = smt[h, 0, PER * t + i]
                parts.append(vhl[m])
                shifts.append(shift[m])
            p2 = lax.dot_general(
                jnp.concatenate(parts, axis=0), xh[h, at, :], (((1,), (1,)), ((), ())),
                preferred_element_type=F32,
            )
            out = jnp.zeros((DIRS, TILE), F32)
            for i in range(PER):
                a = 2 * DIRS * i
                p = p2[a : a + DIRS] + p2[a + DIRS : a + 2 * DIRS]
                p = p - jnp.concatenate([shifts[i], shifts[i]], axis=1)
                out = jnp.where(group == i, p, out)
            pc[h, :, at] = out

        def body(t, carry):
            one(2 * t)
            one(2 * t + 1)
            return carry

        lax.fori_loop(0, TILES // 2, body, 0)

    def p_copy(h):
        return send(pc.at[h], pr.at[h], p_s.at[h], p_r.at[h], partner)

    def expand(h):
        def one(t):
            at = pl.ds(pl.multiple_of(t * TILE, TILE), TILE)
            p = pc[h, :, at] + pr[h, :, at]
            hi = p.astype(BF16).astype(F32)
            lo = p - hi
            parts = []
            for i in range(PER):
                parts.append(jnp.where(group == i, hi, 0.0).astype(BF16))
                parts.append(jnp.where(group == i, lo, 0.0).astype(BF16))
            w2 = jnp.dot(jnp.concatenate(parts, axis=0), xh[h, at, :], preferred_element_type=F32)
            for i in range(PER):
                a = 2 * DIRS * i
                wblk[h, PER * t + i] = w2[a : a + DIRS] + w2[a + DIRS : a + 2 * DIRS]

        def body(t, carry):
            one(2 * t)
            one(2 * t + 1)
            return carry

        lax.fori_loop(0, TILES // 2, body, 0)

    def w_copy(n, d):
        return send(
            wq.at[n, chip_at(d)], rq.at[n, chip], rs_s.at[n, d - 1], rs_r.at[n, d - 1], plane(d)
        )

    def z_copy(step, n, d):
        ref = zq.at[step, n, z]
        return send(ref, ref, z_s.at[step, n, d - 1], z_r.at[step, n, d - 1], column(d))

    def g_copy(n):
        return send(gs.at[n], gr.at[n], g_s.at[n], g_r.at[n], partner)

    def node_total(n, i, first):
        j = 2 * i + n
        w = total(wblk, j)
        if first:
            off = shift0[j] + shift1[j]
            w = w - jnp.concatenate([off * snode[i, n, k : k + 1, :] for k in range(KT)], axis=1)
        return w

    def scatter_start(n, first):
        def go(d):
            put(wq.at[n, chip_at(d)], node_total(n, chip_at(d), first))
            w_copy(n, d).start()

        each(CHIPS, go)
        put(rq.at[n, chip], node_total(n, chip, first))

    def term(ref):
        scale = scale_of(ref)
        return tuple(ref[k].astype(I32).astype(F32) * scale for k in range(KT))

    def plane_total(n):
        def body(d, acc):
            w_copy(n, d).wait_recv()
            return tuple(a + b for a, b in zip(acc, term(rq.at[n, chip_from(d)])))

        return jnp.concatenate(lax.fori_loop(1, CHIPS, body, term(rq.at[n, chip])), axis=1)

    def column_total(step, n):
        acc = term(zq.at[step, n, 0])
        for i in range(1, NZ):
            acc = tuple(a + b for a, b in zip(acc, term(zq.at[step, n, i])))
        return jnp.concatenate(acc, axis=1)

    row_id = lax.broadcasted_iota(I32, (DIRS, 1), 0)

    def orthonormal(g, w):
        scale = jnp.zeros((DIRS, 1), F32)
        for k in range(0, DIRS, 2):
            c0, c1 = g[:, k : k + 1], g[:, k + 1 : k + 2]
            p, q, r = c0[k : k + 1], c0[k + 1 : k + 2], c1[k + 1 : k + 2]
            inv = 1.0 / p
            low = q * inv
            pivot = r - q * low
            f1 = (c1 - low * c0) / pivot
            f0 = c0 * inv - low * f1
            below = row_id > k + 1
            f0 = jnp.where(below, f0, jnp.where(row_id == k + 1, low, 0.0))
            f1 = jnp.where(below, f1, 0.0)
            scale = jnp.where(row_id == k, 1.0 / jnp.sqrt(p), scale)
            scale = jnp.where(row_id == k + 1, 1.0 / jnp.sqrt(pivot), scale)
            g = g - f0 * g[k : k + 1, :] - f1 * g[k + 1 : k + 2, :]
            w = w - f0 * w[k : k + 1, :] - f1 * w[k + 1 : k + 2, :]
        return w * scale

    def one_pass(step, first):
        receive(first)
        for h in range(2):
            project(h)
            p_copy(h).start()
        for n in range(2):
            each(CHIPS, lambda d: v_copy(n, d).wait_send())
        if first:
            sums_to_column()
        for h in range(2):
            p_copy(h).wait_recv()
            expand(h)
        if first:
            means_to_plane()
            offsets()
            over_h.start()
            over_h.wait_recv()
        for n in range(2):
            scatter_start(n, first)
        for n in range(2):
            put(zq.at[step, n, z], plane_total(n))
            each(NZ, lambda d: z_copy(step, n, d).start())
        ws = []
        for n in range(2):
            each(NZ, lambda d: z_copy(step, n, d).wait_recv())
            size = mm[chip, n, KT : KT + 1, :]
            w = column_total(step, n) / jnp.concatenate([size] * KT, axis=1)
            ws.append(w)
            gs[n, :, 0:DIRS] = lax.dot_general(
                w, w, (((1,), (1,)), ((), ())), precision=lax.Precision.HIGHEST,
                preferred_element_type=F32,
            )
            g_copy(n).start()
        for n in range(2):
            g_copy(n).wait_recv()
            v = orthonormal(gs[n, :, 0:DIRS] + gr[n, :, 0:DIRS], ws[n])
            vout[n] = v
            put(vq.at[n, chip], v)
            gather_start(n)
        for n in range(2):
            p_copy(n).wait_send()
            g_copy(n).wait_send()
            each(CHIPS, lambda d: w_copy(n, d).wait_send())
            each(NZ, lambda d: z_copy(step, n, d).wait_send())

    one_pass(0, True)

    def later(step, carry):
        one_pass(step, False)
        return carry

    lax.fori_loop(1, PASSES, later, 0)

    over_o = send(vout.at[other], vin, o_s, o_r, partner)
    over_o.start()
    dirs[:, mine] = vout[c]
    receive(False)
    project(other)
    p_copy(other).start()
    project(c)
    over_o.wait_recv()
    dirs[:, theirs] = vin[...]
    back = send(pc.at[other], pr.at[c], p_s.at[other], p_r.at[c], partner)
    back.wait_recv()
    coords[...] = (pc[c] + pr[c]).astype(BF16)
    back.wait_send()
    for cp in (over_o, over_v, over_m, over_x, over_h):
        cp.wait_send()
    for n in range(2):
        each(CHIPS, lambda d: v_copy(n, d).wait_send())
    each(CHIPS, lambda d: ms(d).wait_send())
    each(CHIPS, lambda d: ma(d).wait_send())
    each(NZ, lambda d: mz(d).wait_send())


def on_device(embeddings, membership, start):
    member = membership.reshape(1, BLOCKS)
    vmem = pl.BlockSpec(memory_space=pltpu.VMEM)
    hbm = pl.BlockSpec(memory_space=pltpu.HBM)
    dma = pltpu.SemaphoreType.DMA
    dirs, coords = pl.pallas_call(
        kernel,
        out_shape=(
            jax.ShapeDtypeStruct((DIRS, D), F32),
            jax.ShapeDtypeStruct((DIRS, ROWS), BF16),
        ),
        in_specs=[hbm, hbm, hbm],
        out_specs=(vmem, vmem),
        scratch_shapes=[
            pltpu.VMEM((2, ROWS, HALF), BF16),
            pltpu.SMEM((2, 8, LANES), I32),
            pltpu.SMEM((2, 1, BLOCKS), I32),
            pltpu.VMEM((2, 1, BLOCKS), I32),
            pltpu.VMEM((2, 8, LANES), I32),
            pltpu.VMEM((DIRS, D), F32),
            pltpu.VMEM((DIRS, HALF), F32),
            pltpu.VMEM((2, CHIPS, KT + 1, DIRS, LANES), I16),
            pltpu.VMEM((32, 2 * DIRS, HALF), BF16),
            pltpu.VMEM((32, DIRS, LANES), F32),
            pltpu.VMEM((32, DIRS, LANES), F32),
            pltpu.VMEM((32, DIRS, LANES), F32),
            pltpu.VMEM((2, DIRS, ROWS), F32),
            pltpu.VMEM((2, DIRS, ROWS), F32),
            pltpu.VMEM((2, BLOCKS + 1, DIRS, HALF), F32),
            pltpu.VMEM((2, CHIPS, KT + 1, DIRS, LANES), I16),
            pltpu.VMEM((2, CHIPS, KT + 1, DIRS, LANES), I16),
            pltpu.VMEM((PASSES, 2, NZ, KT + 1, DIRS, LANES), I16),
            pltpu.VMEM((2, DIRS, LANES), F32),
            pltpu.VMEM((2, DIRS, LANES), F32),
            pltpu.VMEM((2, DIRS, HALF), F32),
            pltpu.VMEM((DIRS, HALF), F32),
            pltpu.VMEM((2, BLOCKS + 1, 8, LANES), F32),
            pltpu.VMEM((CHIPS, 2, 8, LANES), F32),
            pltpu.VMEM((CHIPS, 2, 8, LANES), F32),
            pltpu.VMEM((NZ, 2, 8, LANES), F32),
            pltpu.VMEM((CHIPS, 2, 8, LANES), F32),
            dma, dma, dma, dma, dma, dma, dma, dma, dma, dma, dma, dma, dma,
            dma((2, 15)), dma((2, 15)),
            dma((2,)), dma((2,)),
            dma((2, 15)), dma((2, 15)),
            dma((PASSES, 2, 7)), dma((PASSES, 2, 7)),
            dma((2,)), dma((2,)),
            dma((15,)), dma((15,)), dma((7,)), dma((7,)), dma((15,)), dma((15,)),
            dma, dma,
        ],
        compiler_params=pltpu.CompilerParams(
            collective_id=0, has_side_effects=True, vmem_limit_bytes=40 * 1024 * 1024
        ),
    )(member, embeddings, start)
    return (dirs[None], coords)


def solution(mesh):
    return jax.shard_map(
        on_device,
        mesh=mesh,
        in_specs=(P(("node", "rows"), None), P(("node", "rows"), None), P("node", None, None)),
        out_specs=(P("node", None, None), P(None, ("node", "rows"))),
        check_vma=False,
    )
```

time: 318 us -> 154 us (0.48)
  Pallas kernels: 0 us -> 148 us
  blocking collectives: 135 us -> 0 us
  waiting for transfers between devices: 79.3 us -> 0 us
  matrix products: 39.5 us -> 0 us
  other arithmetic: 25.8 us -> 0 us
  between operations: 14.9 us -> 0.65 us
  local copies, waits for them, and re-layouts: 15.8 us -> 4.94 us
  starting transfers between devices: 7.57 us -> 0 us
    pallas_call x0 -> x1, Pallas kernels: none -> 148 us  [on_device(): pl.pallas_call(kernel, out_shape=(jax.ShapeDtypeStruct((DIRS, D), F32), j...]
    all_to_all x2 -> x0, blocking collectives: 115 us -> none  [the longest x1 104 us: on_device(): lax.all_to_all(outgoing, 'node', split_axis=0, concat_axis=0, tiled=True)]
    psum x1 -> x0, waiting for transfers between devices: 71.7 us -> none  [on_device(): lax.psum((gram_sum, row_sum, node_size), 'rows')]
    dot_general x10 -> x0, matrix products: 38.7 us -> none  [the longest x1 12.2 us: on_device(): jnp.einsum('kd,srd->skr', vectors, received, precision=lax.Precision.HIGH...]
    psum x1 -> x0, blocking collectives: 19.9 us -> none  [on_device(): lax.psum((gram_sum, row_sum, node_size), 'rows')]
    another operation x15 -> x0, other arithmetic: 12.1 us -> none  [the longest x9 6.5 us: orthonormal(): factor = jnp.linalg.cholesky(square)]
    gather x2 -> x0, local copies, waits for them, and re-layouts: 8.2 us -> none  [the longest x1 7.61 us: on_device(): local[source]]
    all_to_all x1 -> x0, waiting for transfers between devices: 7.67 us -> none  [on_device(): lax.all_to_all(values, 'node', split_axis=0, concat_axis=0, tiled=True)]
  transfers between devices with their start and end apart: 2 -> 0, of which waited for: 2 -> 0; matrix products, arithmetic and copies ran while one was open for 2% -> 0% of each run, Pallas kernels for 0% -> 0%
where the time goes in v2:
time: 154 us
  Pallas kernels  148 us (96%)
  local copies, waits for them, and re-layouts  4.94 us (3%)
    pallas_call x1, Pallas kernels, on_device(): pl.pallas_call(kernel, out_shape=(jax.ShapeDtypeStruct((DIRS, D), F32), j...  148 us
    unnamed x8, local copies, waits for them, and re-layouts  4.94 us

profile of v2, /device:TPU:1, one launch (start us, length us, event | category | flops | bytes accessed | tf_op | source)
XLA Modules:
  0.0 154.0 jit_solution(17012726147260604855)
XLA Ops:
  0.6 0.0 copy-start
  0.6 2.2 %copy-done = bf16[2048,1024]{1,0:T(8,128)(2,1)S(1)} copy-done((bf16[2048,1024]{1,0:T(8,128)(2,1)S(1)}, bf16[2048,1024]{1,0:T(8,128)(2,1)}, u32[]{:S(2)}) %copy-start) | copy-done | bytes 4194328
  2.8 0.0 copy-start.1
  2.8 0.8 copy-done.1
  3.7 0.0 copy-start.2
  3.7 0.7 copy-done.2
  4.3 148.4 %shard_map.50 = (f32[16,1024]{1,0:T(8,128)S(1)}, bf16[16,2048]{1,0:T(8,128)(2,1)S(1)}) custom-call(s32[1,32]{1,0:T(1,128)S(1)} %bitcast.3, bf16[2048,1024]{1,0:T(8,128)(2,1)S(1)} %copy-done, f32[1,16,1024]{2,1,0:T(8,128)S(1)} %copy-done.1), custom_call_target="tpu_custom_call" | custom-call | tf_op jit(solution)/shard_map/pallas_call | solution.py:470
  152.7 0.6 copy.7
  153.4 0.6 copy.8
Async XLA Ops:
  0.6 2.2 %copy-start = (bf16[2048,1024]{1,0:T(8,128)(2,1)S(1)}, bf16[2048,1024]{1,0:T(8,128)(2,1)}, u32[]{:S(2)}) copy-start(bf16[2048,1024]{1,0:T(8,128)(2,1)} %x_hbm.1) | copy-start | bytes 12582916
  2.8 0.8 copy-start.1
  3.7 0.7 copy-start.2

commit v3 on v2

v3 whole, which is shorter than its diff:
```python
import jax
import jax.numpy as jnp
from jax import lax
from jax.experimental import pallas as pl
from jax.experimental.pallas import tpu as pltpu
from jax.sharding import PartitionSpec as P

PASSES = 3
MESH = pl.DeviceIdType.MESH
F32 = jnp.float32
BF16 = jnp.bfloat16
I16 = jnp.int16
I32 = jnp.int32

DIRS = 16
D = 1024
HALF = 512
LANES = 128
KT = HALF // LANES
CHUNK = 256
CT = CHUNK // LANES
ROWS = 2048
BLOCK = 64
BLOCKS = 32
TILE = 256
PER = TILE // BLOCK
TILES = ROWS // TILE
CHIPS = 16
NZ = 8


def lane_half():
    return lax.broadcasted_iota(I32, (DIRS, LANES), 1) < LANES // 2


def put(ref, pair):
    exponents = []
    for n, w in enumerate(pair):
        tiles = [w[:, LANES * k : LANES * (k + 1)] for k in range(CT)]
        top = jnp.maximum(jnp.abs(tiles[0]), jnp.abs(tiles[1]))
        top = jnp.maximum(jnp.max(top, axis=1, keepdims=True), 1e-30)
        e = jnp.floor(jnp.log2(top))
        scale = jnp.exp2(14.0 - e)
        for k in range(CT):
            q = jnp.clip(jnp.round(tiles[k] * scale), -32767.0, 32767.0)
            ref[CT * n + k] = q.astype(I32).astype(I16)
        exponents.append(jnp.broadcast_to(e.astype(I32), (DIRS, LANES)))
    ref[2 * CT] = jnp.where(lane_half(), exponents[0], exponents[1]).astype(I16)


def scales_of(ref):
    s = jnp.exp2(ref[2 * CT].astype(I32).astype(F32) - 14.0)
    return [jnp.broadcast_to(s[:, LANES // 2 * n : LANES // 2 * n + 1], (DIRS, LANES)) for n in range(2)]


def kernel(
    member, x_hbm, start, dirs, coords,
    xh, smt, smm, mv, tab, vs, vr, vq, vhl, shift, shift0, shift1, pc, pr, pst, wblk, wq, rq, zq, gs, gr, vout, vin,
    sblk, snode, sr, sz, mm, ds, dr,
    xsem, xs, xr, msem, mss, msr, nsem, tsem, vsem, vss, vsr, h_s, h_r, ag_s, ag_r, p_s, p_r, rs_s, rs_r, z_s, z_r, g_s, g_r,
    ms_s, ms_r, mz_s, mz_r, ma_s, ma_r, d_s, d_r, o_s, o_r,
):
    me = lax.axis_index("node")
    z = lax.axis_index("rows")
    x, y, c = me >> 3, (me >> 1) & 3, me & 1
    chip = me >> 1
    other = 1 - c

    def chip_at(d):
        return (((x + (d >> 2)) & 3) << 2) + ((y + d) & 3)

    def chip_from(d):
        return (((x + 4 - (d >> 2)) & 3) << 2) + ((y + 4 - (d & 3)) & 3)

    def plane(d):
        return (chip_at(d) * 2 + c, z)

    def column(d):
        return (me, (z + d) & (NZ - 1))

    partner = (chip * 2 + other, z)

    def send(src, dst, ssem, rsem, to):
        return pltpu.make_async_remote_copy(
            src_ref=src, dst_ref=dst, send_sem=ssem, recv_sem=rsem, device_id=to, device_id_type=MESH
        )

    def each(n, what):
        if n == NZ:
            for d in range(1, NZ):
                what(d)
        else:
            grouped(lambda ds: [what(d) for d in ds])

    def grouped(what, carry=0):
        def body(g, carry):
            ds = [5 * g + r for r in range(1, 6)]
            if carry_used:
                return what(ds, carry)
            what(ds)
            return carry

        carry_used = not isinstance(carry, int)
        return lax.fori_loop(0, 3, body, carry)

    mine = pl.ds(pl.multiple_of(c * HALF, HALF), HALF)
    theirs = pl.ds(pl.multiple_of(other * HALF, HALF), HALF)
    load = pltpu.make_async_copy(x_hbm.at[:, mine], xh.at[c], xsem)
    load.start()
    load_m = pltpu.make_async_copy(member, mv.at[c], msem)
    load_m.start()
    load_v = pltpu.make_async_copy(start.at[0], vs, vsem)
    load_v.start()

    barrier = pltpu.get_barrier_semaphore()
    pl.semaphore_signal(barrier, inc=1, device_id=partner, device_id_type=MESH)

    def greet_plane(d):
        pl.semaphore_signal(barrier, inc=1, device_id=plane(d), device_id_type=MESH)

    def greet_column(d):
        pl.semaphore_signal(barrier, inc=1, device_id=column(d), device_id_type=MESH)

    each(CHIPS, greet_plane)
    each(NZ, greet_column)

    group = lax.broadcasted_iota(I32, (DIRS, TILE), 1) >> 6
    ones_rows = (lax.broadcasted_iota(I32, (DIRS, TILE), 0) == group).astype(F32).astype(BF16)

    def sum_tiles(h):
        def body(t, carry):
            tile = xh[h, pl.ds(pl.multiple_of(t * TILE, TILE), TILE), :]
            s = jnp.dot(ones_rows, tile, preferred_element_type=F32)
            for i in range(PER):
                rows = [s[i : i + 1, LANES * k : LANES * (k + 1)] for k in range(KT)]
                rows.append(jnp.full((1, LANES), float(BLOCK), F32))
                rows.append(jnp.zeros((3, LANES), F32))
                sblk[h, PER * t + i] = jnp.concatenate(rows, axis=0)
            return carry

        lax.fori_loop(0, TILES, body, 0)

    wblk[0, BLOCKS] = jnp.zeros((DIRS, HALF), F32)
    wblk[1, BLOCKS] = jnp.zeros((DIRS, HALF), F32)
    sblk[0, BLOCKS] = jnp.zeros((8, LANES), F32)
    sblk[1, BLOCKS] = jnp.zeros((8, LANES), F32)
    load_v.wait()
    load_m.wait()
    load.wait()
    sum_tiles(c)

    pl.semaphore_wait(barrier, 1 + (CHIPS - 1) + (NZ - 1))

    over_v = send(vs.at[:, theirs], vr, vss, vsr, partner)
    over_v.start()
    over_m = send(mv.at[c], mv.at[c], mss, msr, partner)
    over_m.start()
    over_x = send(x_hbm.at[:, theirs], xh.at[c], xs, xr, partner)
    over_x.start()

    def v_copy(n, d):
        ref = vq.at[n, chip]
        return send(ref, ref, ag_s.at[n, d - 1], ag_r.at[n, d - 1], plane(d))

    def gather_start(n):
        each(CHIPS, lambda d: v_copy(n, d).start())

    over_v.wait_recv()
    own, pair = vs[:, mine], vr[...]
    for q in range(2):
        at = slice(CHUNK * q, CHUNK * (q + 1))
        put(
            vq.at[q, chip],
            [jnp.where(c == 0, own[:, at], pair[:, at]), jnp.where(c == 0, pair[:, at], own[:, at])],
        )
        gather_start(q)

    over_m.wait_recv()
    names = pltpu.make_async_copy(mv, smm, nsem)
    names.start()
    names.wait()
    lane = lax.broadcasted_iota(I32, (1, LANES), 1)
    for h in range(2):
        low = jnp.full((1, LANES), BLOCKS, I32)
        high = low
        hits = jnp.zeros((1, LANES), I32)
        for b in range(BLOCKS):
            hit = lane == smm[h, 0, b]
            low = jnp.where(hit & (hits == 0), b, low)
            high = jnp.where(hit & (hits > 0), b, high)
            hits = jnp.where(hit, hits + 1, hits)
        row = jnp.concatenate([mv[h], jnp.zeros((1, LANES - BLOCKS), I32)], axis=1)
        tab[h] = jnp.concatenate([row, low, high, jnp.zeros((5, LANES), I32)], axis=0)
    move = pltpu.make_async_copy(tab, smt, tsem)
    move.start()
    over_x.wait_recv()
    sum_tiles(other)
    move.wait()

    def total(ref, j):
        f0, s0 = smt[0, 1, j], smt[0, 2, j]
        f1, s1 = smt[1, 1, j], smt[1, 2, j]
        return (ref[0, f0] + ref[0, s0]) + (ref[1, f1] + ref[1, s1])

    def node_sums(i, carry):
        for n in range(2):
            snode[i, n] = total(sblk, 2 * i + n)
        return carry

    lax.fori_loop(0, CHIPS, node_sums, 0)
    sr[chip] = snode[chip]

    def ms(d):
        return send(snode.at[chip_at(d)], sr.at[chip], ms_s.at[d - 1], ms_r.at[d - 1], plane(d))

    def mz(d):
        return send(sz.at[z], sz.at[z], mz_s.at[d - 1], mz_r.at[d - 1], column(d))

    def ma(d):
        return send(mm.at[chip], mm.at[chip], ma_s.at[d - 1], ma_r.at[d - 1], plane(d))

    each(CHIPS, lambda d: ms(d).start())

    tile_row = lax.broadcasted_iota(I32, (2, 8, LANES), 1)

    def means(a):
        return jnp.where(tile_row < KT, a / jnp.maximum(a[:, KT : KT + 1, :], 1.0), a)

    def plane_sums():
        each(CHIPS, lambda d: ms(d).wait_recv())
        acc = sr[0]
        for i in range(1, CHIPS):
            acc = acc + sr[i]
        sz[z] = acc
        each(NZ, lambda d: mz(d).start())

    def dots(v, a, n):
        out = None
        for k in range(KT):
            part = v[:, LANES * k : LANES * (k + 1)] * a[n, k : k + 1, :]
            out = part if out is None else out + part
        return jnp.sum(out, axis=1, keepdims=True)

    def vector_of(j):
        return vhl[j, 0:DIRS, :].astype(F32) + vhl[j, DIRS : 2 * DIRS, :].astype(F32)

    def offsets():
        def body(g, carry):
            for i in (4 * g, 4 * g + 1, 4 * g + 2, 4 * g + 3):
                a = means(snode[i])
                for n in range(2):
                    shift0[2 * i + n] = jnp.broadcast_to(dots(vector_of(2 * i + n), a, n), (DIRS, LANES))
            return carry

        lax.fori_loop(0, CHIPS // 4, body, 0)

    over_h = send(shift0, shift1, h_s, h_r, partner)
    over_d = send(ds, dr, d_s, d_r, partner)

    def scatter_of(d, first_lane, parts, whole, n):
        count = [part[n, KT : KT + 1, 0:1] for part in parts]
        centre = jnp.zeros((DIRS, 1), F32)
        for i, t in enumerate(count):
            centre = centre + d[:, first_lane + i : first_lane + i + 1] * t
        centre = centre / jnp.maximum(whole[n, KT : KT + 1, 0:1], 1.0)
        m = means(whole)
        out = [jnp.zeros((DIRS, LANES), F32) for _ in range(KT)]
        for i, t in enumerate(count):
            a = means(parts[i])
            weight = (d[:, first_lane + i : first_lane + i + 1] - centre) * t
            for k in range(KT):
                out[k] = out[k] + weight * (a[n, k : k + 1, :] - m[n, k : k + 1, :])
        return jnp.concatenate(out, axis=1)

    def between():
        each(NZ, lambda d: mz(d).wait_recv())
        chips = [sr[i] for i in range(CHIPS)]
        planes = [sz[i] for i in range(NZ)]
        every = planes[0]
        for i in range(1, NZ):
            every = every + planes[i]
        mm[chip] = means(every)
        each(CHIPS, lambda d: ma(d).start())
        lanes = lax.broadcasted_iota(I32, (DIRS, LANES), 1)
        for n in range(2):
            v = vector_of(2 * chip + n)
            out = jnp.zeros((DIRS, LANES), F32)
            for i, part in enumerate(chips + planes):
                out = jnp.where(lanes == i, dots(v, means(part), n), out)
            ds[n] = out
        over_d.start()
        over_d.wait_recv()
        both = [ds[n] + dr[n] for n in range(2)]
        inner = [scatter_of(both[n], 0, chips, sz[z], n) for n in range(2)]
        outer = [scatter_of(both[n], CHIPS, planes, every, n) for n in range(2)]
        return inner, outer

    def convert(q, i, first):
        ref = vq.at[q, i]
        scales = scales_of(ref)
        for n in range(2):
            j = 2 * i + n
            his, los, dots = [], [], None
            for k in range(CT):
                v = ref[CT * n + k].astype(I32)
                hi = ((v >> 8) << 8).astype(F32) * scales[n]
                lo = (v & 255).astype(F32) * scales[n]
                his.append(hi.astype(BF16))
                los.append(lo.astype(BF16))
                if not first:
                    part = (hi + lo) * mm[i, n, CT * q + k : CT * q + k + 1, :]
                    dots = part if dots is None else dots + part
            at = slice(CHUNK * q, CHUNK * (q + 1))
            vhl[j, 0:DIRS, at] = jnp.concatenate(his, axis=1)
            vhl[j, DIRS : 2 * DIRS, at] = jnp.concatenate(los, axis=1)
            if not first:
                dots = jnp.broadcast_to(jnp.sum(dots, axis=1, keepdims=True), (DIRS, LANES))
                shift[j] = dots if q == 0 else shift[j] + dots

    def receive(q, first):
        convert(q, chip, first)

        def arrived(ds):
            for d in ds:
                v_copy(q, d).wait_recv()
            for d in ds:
                convert(q, chip_from(d), first)

        grouped(arrived)

    def project(q, h, first):
        cols = slice(CHUNK * q, CHUNK * (q + 1))

        def one(t):
            at = pl.ds(pl.multiple_of(t * TILE, TILE), TILE)
            parts, shifts = [], []
            for i in range(PER):
                m = smt[h, 0, PER * t + i]
                parts.append(vhl[m, :, cols])
                if q == 1 and not first:
                    shifts.append(shift[m])
            p2 = lax.dot_general(
                jnp.concatenate(parts, axis=0), xh[h, at, cols], (((1,), (1,)), ((), ())),
                preferred_element_type=F32,
            )
            out = jnp.zeros((DIRS, TILE), F32)
            for i in range(PER):
                a = 2 * DIRS * i
                p = p2[a : a + DIRS] + p2[a + DIRS : a + 2 * DIRS]
                if q == 1 and not first:
                    p = p - jnp.concatenate([shifts[i], shifts[i]], axis=1)
                out = jnp.where(group == i, p, out)
            pc[h, :, at] = out if q == 0 else pc[h, :, at] + out

        def body(t, carry):
            one(2 * t)
            one(2 * t + 1)
            return carry

        lax.fori_loop(0, TILES // 2, body, 0)

    def p_copy(h):
        return send(pc.at[h], pr.at[h], p_s.at[h], p_r.at[h], partner)

    def expand(q, h):
        cols = slice(CHUNK * q, CHUNK * (q + 1))

        def one(t):
            at = pl.ds(pl.multiple_of(t * TILE, TILE), TILE)
            if q == 0:
                p = pc[h, :, at] + pr[h, :, at]
                hi = p.astype(BF16).astype(F32)
                lo = p - hi
                parts = []
                for i in range(PER):
                    parts.append(jnp.where(group == i, hi, 0.0).astype(BF16))
                    parts.append(jnp.where(group == i, lo, 0.0).astype(BF16))
                stack = jnp.concatenate(parts, axis=0)
                pst[h, t] = stack
            else:
                stack = pst[h, t]
            w2 = jnp.dot(stack, xh[h, at, cols], preferred_element_type=F32)
            for i in range(PER):
                a = 2 * DIRS * i
                wblk[h, PER * t + i, :, cols] = w2[a : a + DIRS] + w2[a + DIRS : a + 2 * DIRS]

        def body(t, carry):
            one(2 * t)
            one(2 * t + 1)
            return carry

        lax.fori_loop(0, TILES // 2, body, 0)

    def w_copy(n, d):
        return send(
            wq.at[n, chip_at(d)], rq.at[n, chip], rs_s.at[n, d - 1], rs_r.at[n, d - 1], plane(d)
        )

    def z_copy(step, n, d):
        ref = zq.at[step, n, z]
        return send(ref, ref, z_s.at[step, n, d - 1], z_r.at[step, n, d - 1], column(d))

    g_copy = send(gs, gr, g_s, g_r, partner)

    def total_of(j, cols):
        f0, s0 = smt[0, 1, j], smt[0, 2, j]
        f1, s1 = smt[1, 1, j], smt[1, 2, j]
        return (wblk[0, f0, :, cols] + wblk[0, s0, :, cols]) + (
            wblk[1, f1, :, cols] + wblk[1, s1, :, cols]
        )

    def node_totals(q, i, first):
        out = []
        for n in range(2):
            j = 2 * i + n
            w = total_of(j, slice(CHUNK * q, CHUNK * (q + 1)))
            if first:
                off = shift0[j] + shift1[j]
                rows = [snode[i, n, CT * q + k : CT * q + k + 1, :] for k in range(CT)]
                w = w - jnp.concatenate([off * r for r in rows], axis=1)
            out.append(w)
        return out

    def scatter_start(q, first):
        def go(ds):
            for d in ds:
                put(wq.at[q, chip_at(d)], node_totals(q, chip_at(d), first))
            for d in ds:
                w_copy(q, d).start()

        grouped(go)
        put(rq.at[q, chip], node_totals(q, chip, first))

    def term(ref):
        scales = scales_of(ref)
        return tuple(ref[k].astype(I32).astype(F32) * scales[k // CT] for k in range(2 * CT))

    def paired(acc):
        return [jnp.concatenate(acc[CT * n : CT * (n + 1)], axis=1) for n in range(2)]

    def plane_total(q):
        def body(ds, acc):
            for d in ds:
                w_copy(q, d).wait_recv()
            for d in ds:
                acc = tuple(a + b for a, b in zip(acc, term(rq.at[q, chip_from(d)])))
            return acc

        return paired(grouped(body, term(rq.at[q, chip])))

    def column_total(step, q):
        acc = term(zq.at[step, q, 0])
        for i in range(1, NZ):
            acc = tuple(a + b for a, b in zip(acc, term(zq.at[step, q, i])))
        return paired(acc)

    row_id = lax.broadcasted_iota(I32, (DIRS, 1), 0)

    def orthonormal(gw):
        scales = [jnp.zeros((DIRS, 1), F32)] * 2
        for k in range(0, DIRS, 2):
            for n in range(2):
                (g, w), scale = gw[n], scales[n]
                c0, c1 = g[:, k : k + 1], g[:, k + 1 : k + 2]
                p, q, r = c0[k : k + 1], c0[k + 1 : k + 2], c1[k + 1 : k + 2]
                inv = 1.0 / p
                low = q * inv
                pivot = r - q * low
                f1 = (c1 - low * c0) / pivot
                f0 = c0 * inv - low * f1
                below = row_id > k + 1
                f0 = jnp.where(below, f0, jnp.where(row_id == k + 1, low, 0.0))
                f1 = jnp.where(below, f1, 0.0)
                scale = jnp.where(row_id == k, 1.0 / jnp.sqrt(p), scale)
                scales[n] = jnp.where(row_id == k + 1, 1.0 / jnp.sqrt(pivot), scale)
                g = g - f0 * g[k : k + 1, :] - f1 * g[k + 1 : k + 2, :]
                w = w - f0 * w[k : k + 1, :] - f1 * w[k + 1 : k + 2, :]
                gw[n] = (g, w)
        return [gw[n][1] * scales[n] for n in range(2)]

    def one_pass(step, first):
        for q in range(2):
            receive(q, first)
            if first and q == 1:
                offsets()
                over_h.start()
            for h in range(2):
                project(q, h, first)
                if q == 1:
                    p_copy(h).start()
            if first and q == 0:
                plane_sums()
        for q in range(2):
            each(CHIPS, lambda d: v_copy(q, d).wait_send())
        for h in range(2):
            p_copy(h).wait_recv()
            expand(0, h)
        if first:
            over_h.wait_recv()
        scatter_start(0, first)
        for h in range(2):
            expand(1, h)
        scatter_start(1, first)
        if first:
            inner, outer = between()
        for q in range(2):
            total = plane_total(q)
            if first:
                total = [total[n] + inner[n][:, CHUNK * q : CHUNK * (q + 1)] for n in range(2)]
            put(zq.at[step, q, z], total)
            each(NZ, lambda d: z_copy(step, q, d).start())
        halves = []
        for q in range(2):
            each(NZ, lambda d: z_copy(step, q, d).wait_recv())
            halves.append(column_total(step, q))
        ws = []
        for n in range(2):
            w = jnp.concatenate([halves[0][n], halves[1][n]], axis=1)
            if first:
                w = w + outer[n]
            w = w / jnp.concatenate([mm[chip, n, KT : KT + 1, :]] * KT, axis=1)
            ws.append(w)
            gs[n, :, 0:DIRS] = lax.dot_general(
                w, w, (((1,), (1,)), ((), ())), precision=lax.Precision.HIGHEST,
                preferred_element_type=F32,
            )
        g_copy.start()
        g_copy.wait_recv()
        vectors = orthonormal([(gs[n, :, 0:DIRS] + gr[n, :, 0:DIRS], ws[n]) for n in range(2)])
        for q in range(2):
            put(vq.at[q, chip], [v[:, CHUNK * q : CHUNK * (q + 1)] for v in vectors])
            gather_start(q)
        for n in range(2):
            vout[n] = vectors[n]
        if first:
            each(CHIPS, lambda d: ma(d).wait_recv())
        g_copy.wait_send()
        for n in range(2):
            p_copy(n).wait_send()
            each(CHIPS, lambda d: w_copy(n, d).wait_send())
            each(NZ, lambda d: z_copy(step, n, d).wait_send())

    one_pass(0, True)

    def later(step, carry):
        one_pass(step, False)
        return carry

    lax.fori_loop(1, PASSES, later, 0)

    over_o = send(vout.at[other], vin, o_s, o_r, partner)
    over_o.start()
    dirs[:, mine] = vout[c]
    for q in range(2):
        receive(q, False)
        project(q, other, False)
        if q == 1:
            p_copy(other).start()
        project(q, c, False)
    over_o.wait_recv()
    dirs[:, theirs] = vin[...]
    back = send(pc.at[other], pr.at[c], p_s.at[other], p_r.at[c], partner)
    back.wait_recv()
    coords[...] = (pc[c] + pr[c]).astype(BF16)
    back.wait_send()
    for cp in (over_o, over_v, over_m, over_x, over_h, over_d):
        cp.wait_send()
    for n in range(2):
        each(CHIPS, lambda d: v_copy(n, d).wait_send())
    each(CHIPS, lambda d: ms(d).wait_send())
    each(CHIPS, lambda d: ma(d).wait_send())
    each(NZ, lambda d: mz(d).wait_send())


def on_device(embeddings, membership, start):
    member = membership.reshape(1, BLOCKS)
    vmem = pl.BlockSpec(memory_space=pltpu.VMEM)
    hbm = pl.BlockSpec(memory_space=pltpu.HBM)
    dma = pltpu.SemaphoreType.DMA
    dirs, coords = pl.pallas_call(
        kernel,
        out_shape=(
            jax.ShapeDtypeStruct((DIRS, D), F32),
            jax.ShapeDtypeStruct((DIRS, ROWS), BF16),
        ),
        in_specs=[hbm, hbm, hbm],
        out_specs=(vmem, vmem),
        scratch_shapes=[
            pltpu.VMEM((2, ROWS, HALF), BF16),
            pltpu.SMEM((2, 8, LANES), I32),
            pltpu.SMEM((2, 1, BLOCKS), I32),
            pltpu.VMEM((2, 1, BLOCKS), I32),
            pltpu.VMEM((2, 8, LANES), I32),
            pltpu.VMEM((DIRS, D), F32),
            pltpu.VMEM((DIRS, HALF), F32),
            pltpu.VMEM((2, CHIPS, KT + 1, DIRS, LANES), I16),
            pltpu.VMEM((32, 2 * DIRS, HALF), BF16),
            pltpu.VMEM((32, DIRS, LANES), F32),
            pltpu.VMEM((32, DIRS, LANES), F32),
            pltpu.VMEM((32, DIRS, LANES), F32),
            pltpu.VMEM((2, DIRS, ROWS), F32),
            pltpu.VMEM((2, DIRS, ROWS), F32),
            pltpu.VMEM((2, TILES, 2 * DIRS * PER, TILE), BF16),
            pltpu.VMEM((2, BLOCKS + 1, DIRS, HALF), F32),
            pltpu.VMEM((2, CHIPS, KT + 1, DIRS, LANES), I16),
            pltpu.VMEM((2, CHIPS, KT + 1, DIRS, LANES), I16),
            pltpu.VMEM((PASSES, 2, NZ, KT + 1, DIRS, LANES), I16),
            pltpu.VMEM((2, DIRS, LANES), F32),
            pltpu.VMEM((2, DIRS, LANES), F32),
            pltpu.VMEM((2, DIRS, HALF), F32),
            pltpu.VMEM((DIRS, HALF), F32),
            pltpu.VMEM((2, BLOCKS + 1, 8, LANES), F32),
            pltpu.VMEM((CHIPS, 2, 8, LANES), F32),
            pltpu.VMEM((CHIPS, 2, 8, LANES), F32),
            pltpu.VMEM((NZ, 2, 8, LANES), F32),
            pltpu.VMEM((CHIPS, 2, 8, LANES), F32),
            pltpu.VMEM((2, DIRS, LANES), F32),
            pltpu.VMEM((2, DIRS, LANES), F32),
            dma, dma, dma, dma, dma, dma, dma, dma, dma, dma, dma, dma, dma,
            dma((2, 15)), dma((2, 15)),
            dma((2,)), dma((2,)),
            dma((2, 15)), dma((2, 15)),
            dma((PASSES, 2, 7)), dma((PASSES, 2, 7)),
            dma, dma,
            dma((15,)), dma((15,)), dma((7,)), dma((7,)), dma((15,)), dma((15,)),
            dma, dma, dma, dma,
        ],
        compiler_params=pltpu.CompilerParams(
            collective_id=0, has_side_effects=True, vmem_limit_bytes=52 * 1024 * 1024
        ),
    )(member, embeddings, start)
    return (dirs[None], coords)


def solution(mesh):
    return jax.shard_map(
        on_device,
        mesh=mesh,
        in_specs=(P(("node", "rows"), None), P(("node", "rows"), None), P("node", None, None)),
        out_specs=(P("node", None, None), P(None, ("node", "rows"))),
        check_vma=False,
    )
```

time: 154 us -> 143 us (0.929)
  Pallas kernels: 148 us -> 139 us
  local copies, waits for them, and re-layouts: 4.94 us -> 2.75 us
    pallas_call x1, Pallas kernels: 148 us -> 139 us  [on_device(): pl.pallas_call(kernel, out_shape=(jax.ShapeDtypeStruct((DIRS, D), F32), j...]
    unnamed x8 -> x6, local copies, waits for them, and re-layouts: 4.94 us -> 2.75 us
where the time goes in v3:
time: 143 us; the launch traced here: 142 us
  Pallas kernels  139 us (97%)
  local copies, waits for them, and re-layouts  2.75 us (2%)
    pallas_call x1, Pallas kernels, on_device(): pl.pallas_call(kernel, out_shape=(jax.ShapeDtypeStruct((DIRS, D), F32), j...  139 us

profile of v3, /device:TPU:1, one launch (start us, length us, event | category | flops | bytes accessed | tf_op | source)
XLA Modules:
  0.0 142.4 jit_solution(13971331962532105405)
XLA Ops:
  0.6 0.0 copy-start
  0.6 0.8 copy-done
  1.5 0.0 copy-start.1
  1.5 0.7 copy-done.1
  2.1 139.0 %shard_map.50 = (f32[16,1024]{1,0:T(8,128)S(1)}, bf16[16,2048]{1,0:T(8,128)(2,1)S(1)}) custom-call(s32[1,32]{1,0:T(1,128)S(1)} %bitcast.3, bf16[2048,1024]{1,0:T(8,128)(2,1)} %x_hbm.1, f32[1,16,1024]{2,1,0:T(8,128)S(1)} %copy-done), custom_call_target="tpu_custom_call" | custom-call | tf_op jit(solution)/shard_map/pallas_call | solution.py:580
  141.1 0.6 copy.7
  141.7 0.6 copy.8
Async XLA Ops:
  0.6 0.8 copy-start
  1.5 0.7 copy-start.1

commit v4 on v3

--- a/solution.py
+++ b/solution.py
@@ -27,6 +27,7 @@
 TILES = ROWS // TILE
 CHIPS = 16
 NZ = 8
+FAR_FIRST = (10, 6, 9, 11, 14, 5, 7, 13, 15, 2, 8, 1, 3, 4, 12)
 
 
 def lane_half():
@@ -48,6 +49,24 @@
     ref[2 * CT] = jnp.where(lane_half(), exponents[0], exponents[1]).astype(I16)
 
 
+def put_whole(ref, chip, pair):
+    exponents = []
+    for n, w in enumerate(pair):
+        tiles = [w[:, LANES * k : LANES * (k + 1)] for k in range(KT)]
+        top = jnp.maximum(
+            jnp.maximum(jnp.abs(tiles[0]), jnp.abs(tiles[1])),
+            jnp.maximum(jnp.abs(tiles[2]), jnp.abs(tiles[3])),
+        )
+        top = jnp.maximum(jnp.max(top, axis=1, keepdims=True), 1e-30)
+        e = jnp.floor(jnp.log2(top))
+        scale = jnp.exp2(14.0 - e)
+        for k in range(KT):
+            q = jnp.clip(jnp.round(tiles[k] * scale), -32767.0, 32767.0)
+            ref[k // CT, chip, CT * n + k % CT] = q.astype(I32).astype(I16)
+        exponents.append(jnp.broadcast_to(e.astype(I32), (DIRS, LANES)))
+    ref[0, chip, 2 * CT] = jnp.where(lane_half(), exponents[0], exponents[1]).astype(I16)
+
+
 def scales_of(ref):
     s = jnp.exp2(ref[2 * CT].astype(I32).astype(F32) - 14.0)
     return [jnp.broadcast_to(s[:, LANES // 2 * n : LANES // 2 * n + 1], (DIRS, LANES)) for n in range(2)]
@@ -94,7 +113,10 @@
 
     def grouped(what, carry=0):
         def body(g, carry):
-            ds = [5 * g + r for r in range(1, 6)]
+            ds = [
+                jnp.where(g == 0, FAR_FIRST[r], jnp.where(g == 1, FAR_FIRST[r + 5], FAR_FIRST[r + 10]))
+                for r in range(5)
+            ]
             if carry_used:
                 return what(ds, carry)
             what(ds)
@@ -146,8 +168,6 @@
     sblk[1, BLOCKS] = jnp.zeros((8, LANES), F32)
     load_v.wait()
     load_m.wait()
-    load.wait()
-    sum_tiles(c)
 
     pl.semaphore_wait(barrier, 1 + (CHIPS - 1) + (NZ - 1))
 
@@ -159,7 +179,7 @@
     over_x.start()
 
     def v_copy(n, d):
-        ref = vq.at[n, chip]
+        ref = vq.at[n, chip] if n == 0 else vq.at[n, chip, pl.ds(0, 2 * CT)]
         return send(ref, ref, ag_s.at[n, d - 1], ag_r.at[n, d - 1], plane(d))
 
     def gather_start(n):
@@ -167,14 +187,12 @@
 
     over_v.wait_recv()
     own, pair = vs[:, mine], vr[...]
+    put_whole(vq, chip, [jnp.where(c == 0, own, pair), jnp.where(c == 0, pair, own)])
     for q in range(2):
-        at = slice(CHUNK * q, CHUNK * (q + 1))
-        put(
-            vq.at[q, chip],
-            [jnp.where(c == 0, own[:, at], pair[:, at]), jnp.where(c == 0, pair[:, at], own[:, at])],
-        )
         gather_start(q)
 
+    load.wait()
+    sum_tiles(c)
     over_m.wait_recv()
     names = pltpu.make_async_copy(mv, smm, nsem)
     names.start()
@@ -297,7 +315,7 @@
 
     def convert(q, i, first):
         ref = vq.at[q, i]
-        scales = scales_of(ref)
+        scales = scales_of(vq.at[0, i])
         for n in range(2):
             j = 2 * i + n
             his, los, dots = [], [], None
@@ -456,27 +474,27 @@
 
     row_id = lax.broadcasted_iota(I32, (DIRS, 1), 0)
 
-    def orthonormal(gw):
-        scales = [jnp.zeros((DIRS, 1), F32)] * 2
-        for k in range(0, DIRS, 2):
+    def orthonormal(grams, ws):
+        row = lax.broadcasted_iota(I32, (DIRS, LANES), 0)
+        cols = [
+            [jnp.broadcast_to(g[:, k : k + 1], (DIRS, LANES)) for k in range(DIRS)] for g in grams
+        ]
+        tiles = [[w[:, LANES * k : LANES * (k + 1)] for k in range(KT)] for w in ws]
+        pivots = [jnp.ones((DIRS, LANES), F32) for _ in ws]
+        for k in range(DIRS):
             for n in range(2):
-                (g, w), scale = gw[n], scales[n]
-                c0, c1 = g[:, k : k + 1], g[:, k + 1 : k + 2]
-                p, q, r = c0[k : k + 1], c0[k + 1 : k + 2], c1[k + 1 : k + 2]
-                inv = 1.0 / p
-                low = q * inv
-                pivot = r - q * low
-                f1 = (c1 - low * c0) / pivot
-                f0 = c0 * inv - low * f1
-                below = row_id > k + 1
-                f0 = jnp.where(below, f0, jnp.where(row_id == k + 1, low, 0.0))
-                f1 = jnp.where(below, f1, 0.0)
-                scale = jnp.where(row_id == k, 1.0 / jnp.sqrt(p), scale)
-                scales[n] = jnp.where(row_id == k + 1, 1.0 / jnp.sqrt(pivot), scale)
-                g = g - f0 * g[k : k + 1, :] - f1 * g[k + 1 : k + 2, :]
-                w = w - f0 * w[k : k + 1, :] - f1 * w[k + 1 : k + 2, :]
-                gw[n] = (g, w)
-        return [gw[n][1] * scales[n] for n in range(2)]
+                col = cols[n]
+                pivot = col[k][k : k + 1, :]
+                pivots[n] = jnp.where(row == k, pivot, pivots[n])
+                f = jnp.where(row > k, col[k] * (1.0 / pivot), 0.0)
+                for j in range(k + 1, DIRS):
+                    col[j] = col[j] - f * col[j][k : k + 1, :]
+                tiles[n] = [t - f * t[k : k + 1, :] for t in tiles[n]]
+        out = []
+        for n in range(2):
+            scale = 1.0 / jnp.sqrt(pivots[n])
+            out.append(jnp.concatenate([t * scale for t in tiles[n]], axis=1))
+        return out
 
     def one_pass(step, first):
         for q in range(2):
@@ -490,8 +508,6 @@
                     p_copy(h).start()
             if first and q == 0:
                 plane_sums()
-        for q in range(2):
-            each(CHIPS, lambda d: v_copy(q, d).wait_send())
         for h in range(2):
             p_copy(h).wait_recv()
             expand(0, h)
@@ -501,6 +517,8 @@
         for h in range(2):
             expand(1, h)
         scatter_start(1, first)
+        for q in range(2):
+            each(CHIPS, lambda d: v_copy(q, d).wait_send())
         if first:
             inner, outer = between()
         for q in range(2):
@@ -526,9 +544,9 @@
             )
         g_copy.start()
         g_copy.wait_recv()
-        vectors = orthonormal([(gs[n, :, 0:DIRS] + gr[n, :, 0:DIRS], ws[n]) for n in range(2)])
+        vectors = orthonormal([gs[n, :, 0:DIRS] + gr[n, :, 0:DIRS] for n in range(2)], ws)
+        put_whole(vq, chip, vectors)
         for q in range(2):
-            put(vq.at[q, chip], [v[:, CHUNK * q : CHUNK * (q + 1)] for v in vectors])
             gather_start(q)
         for n in range(2):
             vout[n] = vectors[n]

time: 143 us -> 135 us (0.944)
  Pallas kernels: 139 us -> 131 us
    pallas_call x1, Pallas kernels: 139 us -> 131 us  [on_device(): pl.pallas_call(kernel, out_shape=(jax.ShapeDtypeStruct((DIRS, D), F32), j...]
where the time goes in v4:
time: 135 us; the launch traced here: 134 us
  Pallas kernels  131 us (97%)
  local copies, waits for them, and re-layouts  2.75 us (2%)
    pallas_call x1, Pallas kernels, on_device(): pl.pallas_call(kernel, out_shape=(jax.ShapeDtypeStruct((DIRS, D), F32), j...  131 us
    unnamed x6, local copies, waits for them, and re-layouts  2.75 us

profile of v4, /device:TPU:1, one launch (start us, length us, event | category | flops | bytes accessed | tf_op | source)
XLA Modules:
  0.0 134.4 jit_solution(13883532343799519458)
XLA Ops:
  0.6 0.0 copy-start
  0.6 0.8 copy-done
  1.5 0.0 copy-start.1
  1.5 0.7 copy-done.1
  2.1 131.0 %shard_map.50 = (f32[16,1024]{1,0:T(8,128)S(1)}, bf16[16,2048]{1,0:T(8,128)(2,1)S(1)}) custom-call(s32[1,32]{1,0:T(1,128)S(1)} %bitcast.3, bf16[2048,1024]{1,0:T(8,128)(2,1)} %x_hbm.1, f32[1,16,1024]{2,1,0:T(8,128)S(1)} %copy-done), custom_call_target="tpu_custom_call" | custom-call | tf_op jit(solution)/shard_map/pallas_call | solution.py:598
  133.2 0.6 copy.7
  133.8 0.6 copy.8
Async XLA Ops:
  0.6 0.8 copy-start
  1.5 0.7 copy-start.1

commit v5 on v4

--- a/solution.py
+++ b/solution.py
@@ -106,27 +106,34 @@
 
     def each(n, what):
         if n == NZ:
-            for d in range(1, NZ):
+            for d in (4, 3, 5, 2, 6, 1, 7):
                 what(d)
         else:
             grouped(lambda ds: [what(d) for d in ds])
 
-    def grouped(what, carry=0):
-        def body(g, carry):
-            ds = [
-                jnp.where(g == 0, FAR_FIRST[r], jnp.where(g == 1, FAR_FIRST[r + 5], FAR_FIRST[r + 10]))
-                for r in range(5)
-            ]
-            if carry_used:
-                return what(ds, carry)
-            what(ds)
-            return carry
-
-        carry_used = not isinstance(carry, int)
-        return lax.fori_loop(0, 3, body, carry)
+    def grouped(what, carry=0, order=FAR_FIRST):
+        for g in range(0, CHIPS - 1, 5):
+            ds = order[g : g + 5]
+            if isinstance(carry, int):
+                what(ds)
+            else:
+                carry = what(ds, carry)
+        return carry
 
     mine = pl.ds(pl.multiple_of(c * HALF, HALF), HALF)
     theirs = pl.ds(pl.multiple_of(other * HALF, HALF), HALF)
+    barrier = pltpu.get_barrier_semaphore()
+
+    def greet_plane(d):
+        pl.semaphore_signal(barrier, inc=1, device_id=plane(d), device_id_type=MESH)
+
+    def greet_column(d):
+        pl.semaphore_signal(barrier, inc=1, device_id=column(d), device_id_type=MESH)
+
+    each(NZ, greet_column)
+    each(CHIPS, greet_plane)
+    pl.semaphore_signal(barrier, inc=1, device_id=partner, device_id_type=MESH)
+
     load = pltpu.make_async_copy(x_hbm.at[:, mine], xh.at[c], xsem)
     load.start()
     load_m = pltpu.make_async_copy(member, mv.at[c], msem)
@@ -134,17 +141,6 @@
     load_v = pltpu.make_async_copy(start.at[0], vs, vsem)
     load_v.start()
 
-    barrier = pltpu.get_barrier_semaphore()
-    pl.semaphore_signal(barrier, inc=1, device_id=partner, device_id_type=MESH)
-
-    def greet_plane(d):
-        pl.semaphore_signal(barrier, inc=1, device_id=plane(d), device_id_type=MESH)
-
-    def greet_column(d):
-        pl.semaphore_signal(barrier, inc=1, device_id=column(d), device_id_type=MESH)
-
-    each(CHIPS, greet_plane)
-    each(NZ, greet_column)
 
     group = lax.broadcasted_iota(I32, (DIRS, TILE), 1) >> 6
     ones_rows = (lax.broadcasted_iota(I32, (DIRS, TILE), 0) == group).astype(F32).astype(BF16)
@@ -344,13 +340,13 @@
             for d in ds:
                 convert(q, chip_from(d), first)
 
-        grouped(arrived)
+        grouped(arrived, order=FAR_FIRST[::-1])
 
     def project(q, h, first):
         cols = slice(CHUNK * q, CHUNK * (q + 1))
 
         def one(t):
-            at = pl.ds(pl.multiple_of(t * TILE, TILE), TILE)
+            at = pl.ds(t * TILE, TILE)
             parts, shifts = [], []
             for i in range(PER):
                 m = smt[h, 0, PER * t + i]
@@ -370,12 +366,8 @@
                 out = jnp.where(group == i, p, out)
             pc[h, :, at] = out if q == 0 else pc[h, :, at] + out
 
-        def body(t, carry):
-            one(2 * t)
-            one(2 * t + 1)
-            return carry
-
-        lax.fori_loop(0, TILES // 2, body, 0)
+        for t in range(TILES):
+            one(t)
 
     def p_copy(h):
         return send(pc.at[h], pr.at[h], p_s.at[h], p_r.at[h], partner)
@@ -402,12 +394,8 @@
                 a = 2 * DIRS * i
                 wblk[h, PER * t + i, :, cols] = w2[a : a + DIRS] + w2[a + DIRS : a + 2 * DIRS]
 
-        def body(t, carry):
-            one(2 * t)
-            one(2 * t + 1)
-            return carry
-
-        lax.fori_loop(0, TILES // 2, body, 0)
+        for t in range(TILES):
+            one(t)
 
     def w_copy(n, d):
         return send(
@@ -464,7 +452,7 @@
                 acc = tuple(a + b for a, b in zip(acc, term(rq.at[q, chip_from(d)])))
             return acc
 
-        return paired(grouped(body, term(rq.at[q, chip])))
+        return paired(grouped(body, term(rq.at[q, chip]), FAR_FIRST[::-1]))
 
     def column_total(step, q):
         acc = term(zq.at[step, q, 0])
@@ -569,6 +557,11 @@
     over_o = send(vout.at[other], vin, o_s, o_r, partner)
     over_o.start()
     dirs[:, mine] = vout[c]
+    for cp in (over_v, over_m, over_x, over_h, over_d):
+        cp.wait_send()
+    each(CHIPS, lambda d: ms(d).wait_send())
+    each(CHIPS, lambda d: ma(d).wait_send())
+    each(NZ, lambda d: mz(d).wait_send())
     for q in range(2):
         receive(q, False)
         project(q, other, False)
@@ -578,16 +571,12 @@
     over_o.wait_recv()
     dirs[:, theirs] = vin[...]
     back = send(pc.at[other], pr.at[c], p_s.at[other], p_r.at[c], partner)
+    for q in range(2):
+        each(CHIPS, lambda d: v_copy(q, d).wait_send())
     back.wait_recv()
     coords[...] = (pc[c] + pr[c]).astype(BF16)
     back.wait_send()
-    for cp in (over_o, over_v, over_m, over_x, over_h, over_d):
-        cp.wait_send()
-    for n in range(2):
-        each(CHIPS, lambda d: v_copy(n, d).wait_send())
-    each(CHIPS, lambda d: ms(d).wait_send())
-    each(CHIPS, lambda d: ma(d).wait_send())
-    each(NZ, lambda d: mz(d).wait_send())
+    over_o.wait_send()
 
 
 def on_device(embeddings, membership, start):

time: 135 us -> 124 us (0.919)
  Pallas kernels: 131 us -> 121 us
    pallas_call x1, Pallas kernels: 131 us -> 121 us  [on_device(): pl.pallas_call(kernel, out_shape=(jax.ShapeDtypeStruct((DIRS, D), F32), j...]
where the time goes in v5:
time: 124 us
  Pallas kernels  121 us (98%)
  local copies, waits for them, and re-layouts  2.75 us (2%)
    pallas_call x1, Pallas kernels, on_device(): pl.pallas_call(kernel, out_shape=(jax.ShapeDtypeStruct((DIRS, D), F32), j...  121 us
    unnamed x6, local copies, waits for them, and re-layouts  2.75 us

profile of v5, /device:TPU:1, one launch (start us, length us, event | category | flops | bytes accessed | tf_op | source)
XLA Modules:
  0.0 124.1 jit_solution(14102523855707961237)
XLA Ops:
  0.6 0.0 copy-start
  0.6 0.8 copy-done
  1.5 0.0 copy-start.1
  1.5 0.7 copy-done.1
  2.1 120.7 %shard_map.50 = (f32[16,1024]{1,0:T(8,128)S(1)}, bf16[16,2048]{1,0:T(8,128)(2,1)S(1)}) custom-call(s32[1,32]{1,0:T(1,128)S(1)} %bitcast.3, bf16[2048,1024]{1,0:T(8,128)(2,1)} %x_hbm.1, f32[1,16,1024]{2,1,0:T(8,128)S(1)} %copy-done), custom_call_target="tpu_custom_call" | custom-call | tf_op jit(solution)/shard_map/pallas_call | solution.py:587
  122.8 0.6 copy.7
  123.4 0.6 copy.8
Async XLA Ops:
  0.6 0.8 copy-start
  1.5 0.7 copy-start.1
